TPU v7x, 32 devices: a whole 2x2x4 slice. The times are simulated.
32 devices in a mesh: seq: 4 (over y, core), chan: 8 (over z, x).
Axes of the slice: x: 2, y: 2, z: 4, core: 2. Of those that a mesh axis runs over, the one named last changes fastest.
Arguments:
- query_rows: bfloat16 [512, 8192], P('seq', 'chan'), may hold values from -6 to 6
- key_rows: bfloat16 [512, 8192], P('seq', 'chan'), may hold values from -6 to 6
- value_rows: bfloat16 [512, 8192], P('seq', 'chan'), may hold values from -6 to 6
- short_taps: float32 [3, 3, 8192], P(None, None, 'chan'), may hold values from -3.5 to 3.5
- long_filter: float32 [512, 128], P('seq'), may hold values from -1.1 to 1.1
- cotangent: bfloat16 [512, 8192], P('seq', 'chan'), may hold values from -6 to 6
Outputs:
- hyena_out: bfloat16 [512, 8192], P('seq', 'chan')
- grad_query: bfloat16 [512, 8192], P('seq', 'chan')
- grad_key: bfloat16 [512, 8192], P('seq', 'chan')
- grad_value: bfloat16 [512, 8192], P('seq', 'chan')
- grad_filter: float32 [512, 128], P('seq')
All inputs are finite; a program needn't handle non-finite values.
Results may differ from a plain program's by a relative error of at most 0.001.
Values may be sent and summed in bfloat16 or wider, within the bound.
No kernel may reach another device: no remote copies, remote signals or barrier semaphores. Data moves between devices by JAX's collectives and lax.ppermute only.
A program may use at most 64 MiB of HBM per device.

v0:
```python
import functools

import jax
import jax.numpy as jnp
import ml_dtypes
import numpy as np
from jax import lax
from jax.experimental import pallas as pl
from jax.experimental.pallas import tpu as pltpu
from jax.sharding import PartitionSpec as P

F32 = jnp.float32
BF16 = jnp.bfloat16
EDGE = 8
HEAD = 16
VMEM = pl.BlockSpec(memory_space=pltpu.VMEM)
HBM = pl.BlockSpec(memory_space=pltpu.HBM)


def split_table(table):
    high = table.astype(ml_dtypes.bfloat16)
    low = (table - high.astype(np.float64)).astype(ml_dtypes.bfloat16)
    return high, low


def dft_tables(length):
    frequency = np.pi * (2 * np.arange(length) + 1) / (2 * length)
    into = frequency[:, None] * np.arange(length)[None, :]
    high, low = split_table(np.concatenate([np.cos(into), -np.sin(into)], axis=0))
    forward = np.concatenate([high, high, low], axis=1)
    forward = np.pad(forward, ((0, EDGE), (0, 0)))
    back = np.arange(length + EDGE)[:, None] * frequency[None, :]
    high, low = split_table(np.concatenate([np.cos(back), -np.sin(back)], axis=1) / length)
    inverse = np.concatenate([high, high, low], axis=1)
    return jnp.asarray(forward), jnp.asarray(inverse)


def halves(values):
    high = values.astype(BF16)
    return high, (values - high.astype(F32)).astype(BF16)


def table_dot(table, values):
    high, low = halves(values)
    return jnp.dot(
        table, jnp.concatenate([high, low, high], axis=0), preferred_element_type=F32
    )


def tap_sum(rows_ref, first, count, weights):
    total = weights[0:1] * rows_ref[first : first + count]
    for shift in range(1, weights.shape[0]):
        total = total + weights[shift : shift + 1] * rows_ref[first - shift : first - shift + count]
    return total


def put_filter(unit, first, filter_high, filter_low):
    length, groups = filter_high.shape
    width = unit.shape[1]
    rows = length * groups // width
    for tile in range(width // groups):
        lanes = slice(tile * groups, (tile + 1) * groups)
        part = slice(tile * rows, (tile + 1) * rows)
        unit[first : first + rows, lanes] = filter_high[part]
        unit[first + rows : first + 2 * rows, lanes] = filter_low[part]


def get_filter(unit, first, length, groups):
    width = unit.shape[1]
    rows = length * groups // width
    pieces = []
    for tile in range(width // groups):
        lanes = slice(tile * groups, (tile + 1) * groups)
        pieces.append(
            unit[first : first + rows, lanes].astype(F32)
            + unit[first + rows : first + 2 * rows, lanes].astype(F32)
        )
    return jnp.concatenate(pieces, axis=0)


def fetch_kernel(q_hbm, k_hbm, v_hbm, c_hbm, *refs):
    others = refs[:4]
    rows_ref, marks_ref, *other_refs = refs[4:10]
    edge, sems = refs[10:]
    length = q_hbm.shape[0]
    copies = [
        pltpu.make_async_copy(source, rows_ref.at[index], sems.at[index])
        for index, source in enumerate((q_hbm, k_hbm, v_hbm, c_hbm))
    ]
    copies += [
        pltpu.make_async_copy(source, target, sems.at[4 + index])
        for index, (source, target) in enumerate(zip(others, other_refs))
    ]
    for copy in copies:
        copy.start()
    for copy in copies[:4]:
        copy.wait()
    margin = others[0].shape[1] - 1
    edge[...] = jnp.zeros(edge.shape, F32)
    for p in range(4):
        first = rows_ref[p, 0:HEAD].astype(F32)
        edge[(3 + p) * margin : (4 + p) * margin] = first[0:margin]
        if p < 3:
            last = rows_ref[p, length - HEAD :].astype(F32)
            edge[p * margin : (p + 1) * margin] = last[HEAD - margin :]
    marks_ref[...] = edge[...].astype(BF16)
    for copy in copies[4:]:
        copy.wait()


def own_kernel(bits, tile_width, rows_ref, taps_ref, filter_ref, pair_ref, conv_ref, *refs):
    unit_refs, window = refs[:-1], refs[-1]
    length, width = rows_ref.shape[1:]
    half = width // 2
    me = lax.axis_index("seq")
    filter_high, filter_low = halves(filter_ref[...])
    put_filter(pair_ref, 4 * length, filter_high, filter_low)
    for later in unit_refs[1::2]:
        put_filter(later, 2 * length, filter_high, filter_low)
    window[:, 0:EDGE] = jnp.zeros((3, EDGE, tile_width), F32)
    for tile in range(width // tile_width):
        lanes = slice(tile * tile_width, (tile + 1) * tile_width)
        convs = []
        for p in range(3):
            window[p, EDGE:] = rows_ref[p, :, lanes].astype(F32)
            conv = tap_sum(window.at[p], EDGE, length, taps_ref[p, :, lanes])
            conv_ref[p, :, lanes] = conv
            convs.append(conv)
        incoming = rows_ref[3, :, lanes].astype(F32)
        parts = [*halves(convs[1] * convs[2]), *halves(incoming * convs[0])]
        for index, part in enumerate(parts):
            pair_ref[index * length : (index + 1) * length, lanes] = part
        in_half = tile * tile_width // half
        lanes_half = slice(tile * tile_width % half, tile * tile_width % half + tile_width)
        for index, bit in enumerate(bits):
            low_side = (me // bit) % 2 == 0
            first, later = unit_refs[2 * index : 2 * index + 2]
            target_low, target_high = (first, later) if in_half == 0 else (later, first)

            @pl.when(low_side)
            def _():
                target_low[0:length, lanes_half] = parts[0]
                target_low[length : 2 * length, lanes_half] = parts[1]

            @pl.when(jnp.logical_not(low_side))
            def _():
                target_high[0:length, lanes_half] = parts[2]
                target_high[length : 2 * length, lanes_half] = parts[3]


def first_kernel(marks_refs, taps_ref, own_marks, *refs):
    arrived = refs[:marks_refs]
    firsts_ref, conv_ref, after_ref, marks, convs, window = refs[marks_refs:]
    blocks = firsts_ref.shape[0]
    me = lax.axis_index("seq")
    margin = taps_ref.shape[1] - 1
    nothing = jnp.zeros(marks.shape[1:], F32)
    marks[0] = nothing
    marks[blocks + 1] = nothing
    marks[me + 1] = own_marks[...].astype(F32)
    index = 1
    for ref in arrived:
        for place in range(ref.shape[0] // HEAD):
            marks[(me ^ index_of(index, blocks)) + 1] = ref[
                place * HEAD : (place + 1) * HEAD
            ].astype(F32)
            index += 1
    window[...] = jnp.zeros(window.shape, F32)
    convs[blocks] = jnp.zeros(convs.shape[1:], F32)
    for block in range(blocks):
        for p in range(3):
            window[EDGE - margin : EDGE] = marks[block, p * margin : (p + 1) * margin]
            window[EDGE : EDGE + margin] = marks[block + 1, (3 + p) * margin : (4 + p) * margin]
            convs[block, p] = tap_sum(window, EDGE, EDGE, taps_ref[p])
        window[EDGE : EDGE + margin] = marks[block + 1, 6 * margin : 7 * margin]
        firsts_ref[block, 0] = convs[block, 1] * convs[block, 2]
        firsts_ref[block, 1] = window[EDGE:] * convs[block, 0]
    conv_ref[...] = convs[me]
    after_ref[0:2] = convs[me + 1, 1:3]
    window[EDGE : EDGE + margin] = marks[me + 2, 6 * margin : 7 * margin]
    after_ref[2] = window[EDGE:]


def index_of(count, blocks):
    order, bit = [0], blocks // 2
    while bit:
        order += [index ^ bit for index in order]
        bit //= 2
    return order[count]


def with_first(margin, first, rows):
    true = jnp.concatenate([first, jnp.zeros((HEAD - EDGE, first.shape[1]), F32)], axis=0)
    row = lax.broadcasted_iota(jnp.int32, true.shape, 0)
    return jnp.where(row < margin, true, rows)


def spectrum(forward, margin, first, ref, place, lanes):
    length = forward.shape[1] // 3
    parts = []
    for index, part in enumerate(halves(first)):
        begin = place + index * length
        head = with_first(margin, part.astype(F32), ref[begin : begin + HEAD, lanes].astype(F32))
        parts += [head.astype(BF16), ref[begin + HEAD : begin + length, lanes]]
    return jnp.dot(
        forward, jnp.concatenate([*parts, *parts[0:2]], axis=0), preferred_element_type=F32
    )


def cross_add(cross, distance, early, late, groups):
    length = early.shape[0] // 2
    e_re, e_im = early[0:length], early[length:]
    l_re, l_im = late[0:length], late[length:]
    re = e_re * l_re + e_im * l_im
    im = e_re * l_im - e_im * l_re
    parts = range(early.shape[1] // groups)
    cross[distance, 0:length] += sum(re[:, p * groups : (p + 1) * groups] for p in parts)
    cross[distance, length:] += sum(im[:, p * groups : (p + 1) * groups] for p in parts)


def chip_kernel(
    tile_width,
    groups,
    margin,
    own_ref,
    other_ref,
    firsts_ref,
    forward_ref,
    spec_ref,
    cross_ref,
):
    length = forward_ref.shape[1] // 3
    width = own_ref.shape[1]
    me = lax.axis_index("seq")
    core = me % 2
    forward = forward_ref[0 : 2 * length]
    cross_ref[...] = jnp.zeros(cross_ref.shape, F32)

    def one_tile(step, carry):
        lanes = pl.ds(pl.multiple_of(step * tile_width, tile_width), tile_width)
        for ref, slot, block in ((own_ref, core, me), (other_ref, 1 - core, me ^ 1)):
            for kind in range(2):
                first = firsts_ref[block, kind, :, lanes]
                spec_ref[2 * kind + slot, :, lanes] = spectrum(
                    forward, margin, first, ref, 2 * kind * length, lanes
                )
        cross_add(cross_ref, 0, spec_ref[core, :, lanes], spec_ref[2 + core, :, lanes], groups)

        @pl.when(2 * step * tile_width // width == core)
        def _():
            cross_add(cross_ref, 1, spec_ref[0, :, lanes], spec_ref[3, :, lanes], groups)

        return carry

    lax.fori_loop(0, width // tile_width, one_tile, 0)


def filter_grad_kernel(
    blocks,
    tile_width,
    margin,
    spec_ref,
    near_ref,
    firsts_ref,
    forward_ref,
    inverse_ref,
    *refs,
):
    chips = blocks // 2
    units = refs[: chips - 1]
    gf_refs, cross = refs[chips - 1 : -1], refs[-1]
    length = forward_ref.shape[1] // 3
    groups = near_ref.shape[2]
    half = spec_ref.shape[2] // 2
    me = lax.axis_index("seq")
    core, chip = me % 2, me // 2
    forward = forward_ref[0 : 2 * length]
    cross[0:2] = near_ref[...]
    cross[2:] = jnp.zeros((blocks - 1, 2 * length, groups), F32)
    for index, unit in enumerate(units):
        other = chip ^ (index + 1)

        def one_tile(step, carry):
            start = pl.multiple_of(step * tile_width, tile_width)
            lanes = pl.ds(start, tile_width)
            kind = jnp.where(other < chip, 0, 1)
            wide_lanes = pl.ds(pl.multiple_of(kind * half + start, tile_width), tile_width)
            first = firsts_ref[2 * other + core, kind, :, wide_lanes]
            spec = spectrum(forward, margin, first, unit, 0, lanes)

            @pl.when(other < chip)
            def _():
                for slot in range(2):
                    distance = 2 * chip + slot - (2 * other + core)
                    cross_add(cross, distance, spec, spec_ref[2 + slot, :, wide_lanes], groups)

            @pl.when(other > chip)
            def _():
                for slot in range(2):
                    distance = 2 * other + core - (2 * chip + slot)
                    cross_add(cross, distance, spec_ref[slot, :, wide_lanes], spec, groups)

            return carry

        lax.fori_loop(0, half // tile_width, one_tile, 0)

    inverse = inverse_ref[0:length]
    sign = signs(length, groups)
    for place in range(blocks):
        block = me ^ place
        re = cross[block, 0:length] + sign * cross[block + 1, length:]
        im = cross[block, length:] - sign * cross[block + 1, 0:length]
        part = place // chips * 2 + place % 2
        gf_refs[part][place % chips // 2] = table_dot(inverse, jnp.concatenate([re, im], axis=0))


def signs(length, groups):
    row = lax.broadcasted_iota(jnp.int32, (length, groups), 0)
    return jnp.where(row % 2 == 0, 1.0, -1.0)


def result_kernel(blocks, tile_width, tiles, *refs):
    others = blocks // 2 - 1
    (
        rows_ref,
        taps_ref,
        filter_ref,
        conv_ref,
        conv_first,
        firsts_ref,
        after_ref,
        other_ref,
        spec_ref,
        forward_ref,
        inverse_ref,
    ) = refs[:11]
    refs = refs[11:]
    units = [refs[4 * index : 4 * index + 4] for index in range(others)]
    refs = refs[4 * others :]
    if tiles[0] == 0:
        outs, (spectra, filter_rows) = refs[:4], refs[4:6]
        refs = refs[6:]
    else:
        spectra, filter_rows = refs[:2]
        outs = refs[6:10]
        refs = refs[10:]
    acc, fix, grads, rows_out, sems = refs
    length, width = rows_ref.shape[1:]
    groups = filter_ref.shape[1]
    half = width // 2
    margin = taps_ref.shape[1] - 1
    me = lax.axis_index("seq")
    core, chip = me % 2, me // 2
    forward, inverse = forward_ref[0 : 2 * length], inverse_ref[...]

    if tiles[0] == 0:
        sign = signs(length, groups)
        for edge in (0, 1, blocks + 2):
            filter_rows[edge] = jnp.zeros((length, groups), F32)
        filter_rows[me + 2] = filter_ref[...]
        filter_rows[(me ^ 1) + 2] = get_filter(other_ref, 4 * length, length, groups)
        for index, unit in enumerate(units):
            block = me ^ (2 * (index + 1))
            filter_rows[block + 2] = get_filter(unit[1], 2 * length, length, groups)
            filter_rows[(block ^ 1) + 2] = get_filter(unit[3], 2 * length, length, groups)
        previous = None
        for distance in range(blocks):
            own = table_dot(forward, filter_rows[distance + 2])
            if previous is None:
                spectra[distance] = own
            else:
                spectra[distance, 0:length] = own[0:length] - sign * previous[length:]
                spectra[distance, length:] = own[length:] + sign * previous[0:length]
            previous = own

    def wide(values):
        return jnp.concatenate([values] * (tile_width // groups), axis=1)

    def filter_row(block, row):
        return wide(filter_rows[block + 2, pl.ds(row, 1)])

    def add_lower(distance, signal, spec, fresh=False):
        re, im = spec[0:length], spec[length:]
        h_re, h_im = wide(spectra[distance, 0:length]), wide(spectra[distance, length:])
        new_re = h_re * re - h_im * im
        new_im = h_re * im + h_im * re
        acc[0, 0:length] = new_re if fresh else acc[0, 0:length] + new_re
        acc[0, length:] = new_im if fresh else acc[0, length:] + new_im
        near = filter_row(distance + 1, 0) + filter_row(distance - 1, 0)
        far = filter_row(distance + 1, 1) + filter_row(distance - 1, 1)
        fix[0:1] += signal[0:1] * near
        fix[1:2] += signal[0:1] * far + signal[1:2] * near

    def add_upper(distance, signal, spec, fresh=False):
        re, im = spec[0:length], spec[length:]
        h_re, h_im = wide(spectra[distance, 0:length]), wide(spectra[distance, length:])
        new_re = h_re * re + h_im * im
        new_im = h_re * im - h_im * re
        acc[1, 0:length] = new_re if fresh else acc[1, 0:length] + new_re
        acc[1, length:] = new_im if fresh else acc[1, length:] + new_im
        fix[EDGE + 1 : EDGE + 2] += signal[0:1] * (
            filter_row(distance - 2, length - 1) + filter_row(distance, length - 1)
        )

    copies = []
    for count, tile in enumerate(tiles):
        start = tile * tile_width
        in_half = start // half
        lanes = slice(start, start + tile_width)
        lanes_half = slice(start % half, start % half + tile_width)
        lanes_out = slice(count * tile_width, (count + 1) * tile_width)
        weights = [taps_ref[p, :, lanes] for p in range(3)]
        fix[...] = jnp.zeros(fix.shape, F32)

        add_lower(0, firsts_ref[me, 0, :, lanes], spec_ref[core, :, lanes], True)
        add_upper(0, firsts_ref[me, 1, :, lanes], spec_ref[2 + core, :, lanes], True)

        @pl.when(core == 1)
        def _():
            add_lower(1, firsts_ref[me - 1, 0, :, lanes], spec_ref[0, :, lanes])

        @pl.when(core == 0)
        def _():
            add_upper(1, firsts_ref[me + 1, 1, :, lanes], spec_ref[3, :, lanes])

        for index, unit in enumerate(units):
            other = chip ^ (index + 1)
            for side in range(2):
                first, later = unit[2 * side : 2 * side + 2]
                body_low, body_high = (first, later) if in_half == 0 else (later, first)
                block = 2 * other + (core if side == 0 else 1 - core)

                @pl.when(other < chip)
                def _():
                    signal = firsts_ref[block, 0, :, lanes]
                    spec = spectrum(forward, margin, signal, body_low, 0, lanes_half)
                    add_lower(me - block, signal, spec)

                @pl.when(other > chip)
                def _():
                    signal = firsts_ref[block, 1, :, lanes]
                    spec = spectrum(forward, margin, signal, body_high, 0, lanes_half)
                    add_upper(block - me, signal, spec)

        after_key, after_value, after_incoming = [
            after_ref[p, :, lanes][0:margin] for p in range(3)
        ]
        gated = after_key * after_value
        zero_lag, one_lag = filter_row(0, 0), filter_row(0, 1)
        fix[0:1] += gated[0:1] * zero_lag
        fix[1:2] += gated[1:2] * zero_lag + gated[0:1] * one_lag

        long_conv = table_dot(inverse, acc[0])
        gated_grad = table_dot(inverse, acc[1])
        query_conv, key_conv, value_conv = [
            jnp.concatenate(
                [
                    with_first(margin, conv_first[p, :, lanes], conv_ref[p, 0:HEAD, lanes]),
                    conv_ref[p, HEAD:, lanes],
                ],
                axis=0,
            )
            for p in range(3)
        ]
        incoming = rows_ref[3, :, lanes].astype(F32)
        beyond = slice(length, length + margin)
        grad_edge = gated_grad[beyond] + fix[EDGE : EDGE + margin]
        grads[0, 0:length] = incoming * long_conv[0:length]
        grads[0, beyond] = after_incoming * (long_conv[beyond] + fix[0:margin])
        grads[1, 0:length] = gated_grad[0:length] * value_conv
        grads[1, beyond] = grad_edge * after_value
        grads[2, 0:length] = gated_grad[0:length] * key_conv
        grads[2, beyond] = grad_edge * after_key
        rows_out[0, :, lanes_out] = (query_conv * long_conv[0:length]).astype(BF16)
        for p in range(3):
            total = weights[p][0:1] * grads[p, 0:length]
            for shift in range(1, margin + 1):
                total = total + weights[p][shift : shift + 1] * grads[p, shift : shift + length]
            rows_out[1 + p, :, lanes_out] = total.astype(BF16)
        for p, out in enumerate(outs):
            copy = pltpu.make_async_copy(
                rows_out.at[p, :, lanes_out], out.at[:, lanes], sems.at[4 * count + p]
            )
            copy.start()
            copies.append(copy)
    for copy in copies:
        copy.wait()


def per_device(query_rows, key_rows, value_rows, short_taps, long_filter, cotangent):
    length, width = query_rows.shape
    groups = long_filter.shape[1]
    blocks = lax.axis_size("seq")
    chans = lax.axis_size("chan")
    chips, half = blocks // 2, width // 2
    margin = short_taps.shape[1] - 1
    tile_width = min(half, 256)
    bits = []
    while 2 << len(bits) < blocks:
        bits.append(2 << len(bits))
    bits.reverse()
    forward, inverse = dft_tables(length)
    shape = jax.ShapeDtypeStruct

    def swap(block, bit):
        return lax.ppermute(block, "seq", [(i, i ^ bit) for i in range(blocks)])

    def call(kernel, outs, args, scratch, in_specs=None, out_specs=None, aliases={}, cost=1):
        return list(
            pl.pallas_call(
                kernel,
                out_shape=outs,
                in_specs=in_specs or [VMEM] * len(args),
                out_specs=out_specs or [VMEM] * len(outs),
                scratch_shapes=scratch,
                input_output_aliases=aliases,
                compiler_params=pltpu.CompilerParams(vmem_limit_bytes=40 * 1024 * 1024),
                cost_estimate=pl.CostEstimate(flops=1, bytes_accessed=cost, transcendentals=0),
            )(*args)
        )

    def after(value, *others):
        return lax.optimization_barrier((value, *others))[0]

    rows, marks, short_taps, long_filter, forward, inverse = call(
        fetch_kernel,
        [
            shape((4, length, width), BF16),
            shape((HEAD, width), BF16),
            shape(short_taps.shape, F32),
            shape(long_filter.shape, F32),
            shape(forward.shape, BF16),
            shape(inverse.shape, BF16),
        ],
        [
            pltpu.with_memory_space_constraint(array, pltpu.HBM)
            for array in (
                query_rows,
                key_rows,
                value_rows,
                cotangent,
                short_taps,
                long_filter,
                forward,
                inverse,
            )
        ],
        [pltpu.VMEM((HEAD, width), F32), pltpu.SemaphoreType.DMA((8,))],
        [HBM] * 8,
    )
    all_marks = []
    for bit in bits + [1]:
        all_marks.append(swap(jnp.concatenate([marks] + all_marks, axis=0), bit))
    firsts_true, conv_first, after_rows = call(
        functools.partial(first_kernel, len(all_marks)),
        [
            shape((blocks, 2, EDGE, width), F32),
            shape((3, EDGE, width), F32),
            shape((3, EDGE, width), F32),
        ],
        [short_taps, marks, *all_marks],
        [
            pltpu.VMEM((blocks + 2, HEAD, width), F32),
            pltpu.VMEM((blocks + 1, 3, EDGE, width), F32),
            pltpu.VMEM((2 * EDGE, width), F32),
        ],
    )
    filter_rows = length * groups // width
    pair_shape = shape((4 * length + 2 * filter_rows, width), BF16)
    first_shape = shape((2 * length, half), BF16)
    later_shape = shape((2 * length + 4 * filter_rows, half), BF16)
    pair, conv, *own_units = call(
        functools.partial(own_kernel, bits, tile_width),
        [pair_shape, shape((3, length, width), F32)] + [first_shape, later_shape] * len(bits),
        [rows, short_taps, long_filter],
        [pltpu.VMEM((3, EDGE + length, tile_width), F32)],
        cost=40 * length * width,
    )

    def gather(own):
        units = {}
        for bit, block in zip(bits, own):
            arrived = {bit // 2: swap(block, bit)}
            for index, unit in units.items():
                arrived[index ^ bit // 2] = swap(unit, bit)
            units.update(arrived)
        return [units[index] for index in range(1, chips)]

    firsts = gather([after(unit, all_marks[0]) for unit in own_units[0::2]])
    sibling = swap(after(pair, all_marks[0]), 1)
    spec, near = call(
        functools.partial(chip_kernel, tile_width, groups, margin),
        [shape((4, 2 * length, width), F32), shape((2, 2 * length, groups), F32)],
        [pair, sibling, firsts_true, forward],
        [],
    )
    shares = call(
        functools.partial(filter_grad_kernel, blocks, tile_width, margin),
        [shape((blocks // 4, length, groups), F32)] * 4,
        [spec, near, firsts_true, forward, inverse, *firsts],
        [pltpu.VMEM((blocks + 1, 2 * length, groups), F32)],
    )
    laters = gather([after(unit, near) for unit in own_units[1::2]])
    share, sent = shares[0] + swap(shares[1], 1), shares[2] + swap(shares[3], 1)
    for bit in bits:
        share = after(share, *laters) + swap(sent, bit)
        if bit > 2:
            count = share.shape[0] // 2
            share, sent = share[:count], share[count:]
    units = []
    for first, later in zip(firsts, laters):
        units += [first, later, swap(after(first, share), 1), swap(after(later, share), 1)]
    rows_out = shape((length, width), BF16)
    windows = [
        shape((blocks, 2 * length, groups), F32),
        shape((blocks + 3, length, groups), F32),
    ]

    def results(tiles, extra, outs, out_specs):
        args = [rows, short_taps, long_filter, conv, conv_first, firsts_true, after_rows]
        args += [sibling, spec, forward, inverse, *units]
        count = len(args)
        return call(
            functools.partial(result_kernel, blocks, tile_width, tiles),
            outs,
            args + extra,
            [
                pltpu.VMEM((2, 2 * length, tile_width), F32),
                pltpu.VMEM((2 * EDGE, tile_width), F32),
                pltpu.VMEM((3, length + EDGE, tile_width), F32),
                pltpu.VMEM((4, length, len(tiles) * tile_width), BF16),
                pltpu.SemaphoreType.DMA((4 * len(tiles),)),
            ],
            [VMEM] * count + ([VMEM] * 2 + [HBM] * 4 if extra else []),
            out_specs,
            {count + 2 + index: index for index in range(4)} if extra else {},
            80 * length * len(tiles) * tile_width,
        )

    tiles = width // tile_width
    cuts = [0, max(1, tiles // 4), tiles - tiles // 4, tiles]
    *final, spectra, filter_blocks = results(
        range(cuts[0], cuts[1]), [], [rows_out] * 4 + windows, [HBM] * 4 + [VMEM] * 2
    )
    ready = [final]
    for begin, end in zip(cuts[1:], cuts[2:]):
        if begin < end:
            final = results(
                range(begin, end), [spectra, filter_blocks, *final], [rows_out] * 4, [HBM] * 4
            )
        ready.append(final)

    grad_filter = share[0]
    steps = [1 << index for index in range(chans.bit_length() - 1)]
    for index, step in enumerate(steps):
        arrived = lax.ppermute(grad_filter, "chan", [(i, i ^ step) for i in range(chans)])
        beside = index + len(ready) - len(steps)
        if beside >= 0:
            grad_filter = after(grad_filter, ready[beside][0])
        grad_filter = grad_filter + arrived
    return (*final, grad_filter)


def solution(mesh):
    in_specs = (
        P("seq", "chan"),
        P("seq", "chan"),
        P("seq", "chan"),
        P(None, None, "chan"),
        P("seq", None),
        P("seq", "chan"),
    )
    out_specs = (
        P("seq", "chan"),
        P("seq", "chan"),
        P("seq", "chan"),
        P("seq", "chan"),
        P("seq", None),
    )
    return jax.shard_map(
        per_device, mesh=mesh, in_specs=in_specs, out_specs=out_specs, check_vma=False
    )
```

profile of v0, /device:TPU:0, one launch (start us, length us, event | category | flops | bytes accessed | tf_op | source)
XLA Modules:
  0.0 40.2 jit_solution(1328713369977361723)
XLA Ops:
  0.6 1.4 %shard_map.119 = (bf16[4,128,1024]{2,1,0:T(8,128)(2,1)S(1)}, bf16[16,1024]{1,0:T(8,128)(2,1)S(1)}, f32[3,3,1024]{2,1,0:T(4,128)S(1)}, f32[128,128]{1,0:T(8,128)S...) custom-call(bf16[128,1024]{1,0:T(8,128)(2,1)} %q_hbm.1, bf16[128,1024]{1,0:T(8,128)(2,1)} %k_hbm.1, ...), custom_call_target="tpu_custom_call" | custom-call | flops 1 | bytes 1 | tf_op jit(solution)/shard_map/pallas_call | solution.py:510
  2.1 3.0 %collective-permute-start = (bf16[16,1024]{1,0:T(8,128)(2,1)S(1)}, bf16[16,1024]{1,0:T(8,128)(2,1)S(1)}, u32[]{:S(2)}, u32[]{:S(2)}) collective-permute-start(bf16[16,1024]{1,0:T(8,128)(2,1)S(1)} %get-tuple-element.51.own_marks), channel_id=1, source_target_pairs={{0,16},{8,24},{16,0},{24,8},{1,17},{9,25},{17,1},{25,9},{2,18},{10... | collective-permute-start | bytes 98312 | tf_op jit(solution)/shard_map/ppermute | solution.py:506
  5.1 1.1 %shard_map.120 = (bf16[544,1024]{1,0:T(8,128)(2,1)S(1)}, f32[3,128,1024]{2,1,0:T(8,128)S(1)}, bf16[256,512]{1,0:T(8,128)(2,1)S(1)}, bf16[320,512]{1,0:T(8,128)(2,1)S(1)}) custom-call(bf16[4,128,1024]{2,1,0:T(8,128)(2,1)S(1)} %get-tuple-element.47.rows_ref.refs_0_, f32[3,3,1024]{2,1,0:T(4,128)S(1)} %get-tuple-element.48.taps_ref.refs_1_, ...), custom_call_target="tpu_custom_call" | custom-call | flops 1 | bytes 5242880 | tf_op jit(solution)/shard_map/pallas_call | solution.py:510
  6.2 0.8 %collective-permute-done.refs_0_ = bf16[16,1024]{1,0:T(8,128)(2,1)S(1)} collective-permute-done((bf16[16,1024]{1,0:T(8,128)(2,1)S(1)}, bf16[16,1024]{1,0:T(8,128)(2,1)S(1)}, u32[]{:S(2)}, u32[]{:S(2)}) %collective-permute-start) | collective-permute-done | bytes 32800 | tf_op jit(solution)/shard_map/ppermute | solution.py:506
  7.0 0.5 %collective-permute-start.1 = (bf16[32,1024]{1,0:T(8,128)(2,1)S(1)}, bf16[32,1024]{1,0:T(8,128)(2,1)S(1)}, u32[]{:S(2)}, u32[]{:S(2)}) collective-permute-start(bf16[32,1024]{1,0:T(8,128)(2,1)S(1)} %pad_maximum_fusion), channel_id=1, source_target_pairs={{0,8},{8,0},{16,24},{24,16},{1,9},{9,1},{17,25},{25,17},{2,10},{10... | collective-permute-start | bytes 196616 | tf_op jit(solution)/shard_map/ppermute | solution.py:506
  7.5 2.0 %collective-permute-start.3 = (bf16[256,512]{1,0:T(8,128)(2,1)S(1)}, bf16[256,512]{1,0:T(8,128)(2,1)S(1)}, u32[]{:S(2)}, u32[]{:S(2)}) collective-permute-start(bf16[256,512]{1,0:T(8,128)(2,1)S(1)} %get-tuple-element.61), channel_id=1, source_target_pairs={{0,16},{8,24},{16,0},{24,8},{1,17},{9,25},{17,1},{25,9},{2,18},{10... | collective-permute-start | bytes 786440 | tf_op jit(solution)/shard_map/ppermute | solution.py:506
  10.2 2.4 %shard_map.122 = (f32[4,256,1024]{2,1,0:T(8,128)S(1)}, f32[2,256,128]{2,1,0:T(8,128)S(1)}) custom-call(bf16[544,1024]{1,0:T(8,128)(2,1)S(1)} %get-tuple-element.56.own_ref, bf16[544,1024]{1,0:T(8,128)(2,1)S(1)} %collective-permute-done.2.other_ref.refs_7_, f32[4,2,8,1024]{3,2,1,0:T(8,128)S(1)} %get-tuple-element.53.firsts_ref.refs_5_, ...), custom_call_target="tpu_custom_call" | custom-call | flops 1 | bytes 1 | tf_op jit(solution)/shard_map/pallas_call | solution.py:510
  12.6 2.1 %collective-permute-start.4 = (bf16[320,512]{1,0:T(8,128)(2,1)S(1)}, bf16[320,512]{1,0:T(8,128)(2,1)S(1)}, u32[]{:S(2)}, u32[]{:S(2)}) collective-permute-start(bf16[320,512]{1,0:T(8,128)(2,1)S(1)} %get-tuple-element.64), channel_id=1, source_target_pairs={{0,16},{8,24},{16,0},{24,8},{1,17},{9,25},{17,1},{25,9},{2,18},{10... | collective-permute-start | bytes 983048 | tf_op jit(solution)/shard_map/ppermute | solution.py:506
  14.7 1.7 %collective-permute-done.3.refs_0_.refs_11_ = bf16[256,512]{1,0:T(8,128)(2,1)S(1)} collective-permute-done((bf16[256,512]{1,0:T(8,128)(2,1)S(1)}, bf16[256,512]{1,0:T(8,128)(2,1)S(1)}, u32[]{:S(2)}, u32[]{:S(2)}) %collective-permute-start.3) | collective-permute-done | bytes 262176 | tf_op jit(solution)/shard_map/ppermute | solution.py:506
  16.4 1.3 %shard_map.123 = (f32[1,128,128]{2,1,0:T(8,128)S(1)}, f32[1,128,128]{2,1,0:T(8,128)S(1)}, f32[1,128,128]{2,1,0:T(8,128)S(1)}, f32[1,128,128]{2,1,0:T(8,128)S(1)}) custom-call(f32[4,256,1024]{2,1,0:T(8,128)S(1)} %get-tuple-element.58.spec_ref.refs_8_, f32[2,256,128]{2,1,0:T(8,128)S(1)} %get-tuple-element.63.near_ref, ...), custom_call_target="tpu_custom_call" | custom-call | flops 1 | bytes 1 | tf_op jit(solution)/shard_map/pallas_call | solution.py:510
  17.7 0.5 %collective-permute-start.5 = (f32[1,128,128]{2,1,0:T(8,128)S(1)}, f32[1,128,128]{2,1,0:T(8,128)S(1)}, u32[]{:S(2)}, u32[]{:S(2)}) collective-permute-start(f32[1,128,128]{2,1,0:T(8,128)S(1)} %get-tuple-element.66), channel_id=1, source_target_pairs={{0,8},{8,0},{16,24},{24,16},{1,9},{9,1},{17,25},{25,17},{2,10},{10... | collective-permute-start | bytes 196616 | tf_op jit(solution)/shard_map/ppermute | solution.py:506
  18.2 0.7 %collective-permute-done.6 = f32[1,128,128]{2,1,0:T(8,128)S(1)} collective-permute-done((f32[1,128,128]{2,1,0:T(8,128)S(1)}, f32[1,128,128]{2,1,0:T(8,128)S(1)}, u32[]{:S(2)}, u32[]{:S(2)}) %collective-permute-start.6) | collective-permute-done | bytes 65568 | tf_op jit(solution)/shard_map/ppermute | solution.py:506
  19.0 1.8 %collective-permute-start.7 = (f32[1,128,128]{2,1,0:T(8,128)S(1)}, f32[1,128,128]{2,1,0:T(8,128)S(1)}, u32[]{:S(2)}, u32[]{:S(2)}) collective-permute-start(f32[1,128,128]{2,1,0:T(8,128)S(1)} %add.19), channel_id=1, source_target_pairs={{0,16},{8,24},{16,0},{24,8},{1,17},{9,25},{17,1},{25,9},{2,18},{10... | collective-permute-start | bytes 196616 | tf_op jit(solution)/shard_map/ppermute | solution.py:506
  20.8 2.6 %collective-permute-done.4.refs_12_ = bf16[320,512]{1,0:T(8,128)(2,1)S(1)} collective-permute-done((bf16[320,512]{1,0:T(8,128)(2,1)S(1)}, bf16[320,512]{1,0:T(8,128)(2,1)S(1)}, u32[]{:S(2)}, u32[]{:S(2)}) %collective-permute-start.4) | collective-permute-done | bytes 327712 | tf_op jit(solution)/shard_map/ppermute | solution.py:506
  23.4 1.1 %collective-permute-done.7 = f32[1,128,128]{2,1,0:T(8,128)S(1)} collective-permute-done((f32[1,128,128]{2,1,0:T(8,128)S(1)}, f32[1,128,128]{2,1,0:T(8,128)S(1)}, u32[]{:S(2)}, u32[]{:S(2)}) %collective-permute-start.7) | collective-permute-done | bytes 65568 | tf_op jit(solution)/shard_map/ppermute | solution.py:506
  24.6 0.5 %collective-permute-start.8 = (bf16[256,512]{1,0:T(8,128)(2,1)S(1)}, bf16[256,512]{1,0:T(8,128)(2,1)S(1)}, u32[]{:S(2)}, u32[]{:S(2)}) collective-permute-start(bf16[256,512]{1,0:T(8,128)(2,1)S(1)} %collective-permute-done.3.refs_0_.refs_11_), channel_id=1, source_target_pairs={{0,8},{8,0},{16,24},{24,16},{1,9},{9,1},{17,25},{25,17},{2,10},{10... | collective-permute-start | bytes 786440 | tf_op jit(solution)/shard_map/ppermute | solution.py:506
  25.1 1.7 %collective-permute-start.10 = (f32[128,128]{1,0:T(8,128)S(1)}, f32[128,128]{1,0:T(8,128)S(1)}, u32[]{:S(2)}, u32[]{:S(2)}) collective-permute-start(f32[128,128]{1,0:T(8,128)S(1)} %bitcast.1), channel_id=1, source_target_pairs={{0,1},{1,0},{2,3},{3,2},{4,5},{5,4},{6,7},{7,6},{8,9},{9,8},{10,11... | collective-permute-start | bytes 196616 | tf_op jit(solution)/shard_map/ppermute | solution.py:656
  26.8 2.2 %shard_map.124 = (bf16[128,1024]{1,0:T(8,128)(2,1)}, bf16[128,1024]{1,0:T(8,128)(2,1)}, bf16[128,1024]{1,0:T(8,128)(2,1)}, bf16[128,1024]{1,0:T(8,128)(2,1)}, f3...) custom-call(bf16[4,128,1024]{2,1,0:T(8,128)(2,1)S(1)} %get-tuple-element.47.rows_ref.refs_0_, ...), custom_call_target="tpu_custom_call" | custom-call | flops 1 | bytes 2621440 | tf_op jit(solution)/shard_map/pallas_call | solution.py:510
  29.4 1.9 %collective-permute-start.11 = (f32[128,128]{1,0:T(8,128)S(1)}, f32[128,128]{1,0:T(8,128)S(1)}, u32[]{:S(2)}, u32[]{:S(2)}) collective-permute-start(f32[128,128]{1,0:T(8,128)S(1)} %add.21), channel_id=1, source_target_pairs={{0,2},{1,3},{2,0},{3,1},{4,6},{5,7},{6,4},{7,5},{8,10},{9,11},{10,... | collective-permute-start | bytes 196616 | tf_op jit(solution)/shard_map/ppermute | solution.py:656
  31.2 3.0 %shard_map.125 = (bf16[128,1024]{1,0:T(8,128)(2,1)}, bf16[128,1024]{1,0:T(8,128)(2,1)}, bf16[128,1024]{1,0:T(8,128)(2,1)}, bf16[128,1024]{1,0:T(8,128)(2,1)}) custom-call(bf16[4,128,1024]{2,1,0:T(8,128)(2,1)S(1)} %get-tuple-element.47.rows_ref.refs_0_, ...), custom_call_target="tpu_custom_call", output_to_operand_aliasing={{0}: (17, {}), {1}: (18, {}), {2}: (19, {}), {3}: (20, {})} | custom-call | flops 1 | bytes 5242880 | tf_op jit(solution)/shard_map/pallas_call | solution.py:510
  34.3 2.7 %collective-permute-start.12 = (f32[128,128]{1,0:T(8,128)S(1)}, f32[128,128]{1,0:T(8,128)S(1)}, u32[]{:S(2)}, u32[]{:S(2)}) collective-permute-start(f32[128,128]{1,0:T(8,128)S(1)} %add.22), channel_id=1, source_target_pairs={{0,4},{1,5},{2,6},{3,7},{4,0},{5,1},{6,2},{7,3},{8,12},{9,13},{10,... | collective-permute-start | bytes 196616 | tf_op jit(solution)/shard_map/ppermute | solution.py:656
  36.9 1.9 %shard_map.126 = (bf16[128,1024]{1,0:T(8,128)(2,1)}, bf16[128,1024]{1,0:T(8,128)(2,1)}, bf16[128,1024]{1,0:T(8,128)(2,1)}, bf16[128,1024]{1,0:T(8,128)(2,1)}) custom-call(bf16[4,128,1024]{2,1,0:T(8,128)(2,1)S(1)} %get-tuple-element.47.rows_ref.refs_0_, ...), custom_call_target="tpu_custom_call", output_to_operand_aliasing={{0}: (17, {}), {1}: (18, {}), {2}: (19, {}), {3}: (20, {})} | custom-call | flops 1 | bytes 2621440 | tf_op jit(solution)/shard_map/pallas_call | solution.py:510
  38.8 0.7 %collective-permute-done.12 = f32[128,128]{1,0:T(8,128)S(1)} collective-permute-done((f32[128,128]{1,0:T(8,128)S(1)}, f32[128,128]{1,0:T(8,128)S(1)}, u32[]{:S(2)}, u32[]{:S(2)}) %collective-permute-start.12) | collective-permute-done | bytes 65568 | tf_op jit(solution)/shard_map/ppermute | solution.py:656
  39.5 0.6 %add.23 = f32[128,128]{1,0:T(8,128)} add(f32[128,128]{1,0:T(8,128)S(1)} %add.22, f32[128,128]{1,0:T(8,128)S(1)} %collective-permute-done.12) | non-fusion elementwise | flops 16384 | bytes 196608 | tf_op jit(solution)/shard_map/add | solution.py:660
  (17 shorter events, 1.2 us)
Async XLA Ops:
  2.1 4.9 %collective-permute-start = (bf16[16,1024]{1,0:T(8,128)(2,1)S(1)}, bf16[16,1024]{1,0:T(8,128)(2,1)S(1)}, u32[]{:S(2)}, u32[]{:S(2)}) collective-permute-start(bf16[16,1024]{1,0:T(8,128)(2,1)S(1)} %get-tuple-element.51.own_marks), channel_id=1, source_target_pairs={{0,16},{8,24},{16,0},{24,8},{1,17},{9,25},{17,1},{25,9},{2,18},{10... | collective-permute-start | bytes 98312 | tf_op jit(solution)/shard_map/ppermute | solution.py:506
  7.0 3.2 %collective-permute-start.2 = (bf16[544,1024]{1,0:T(8,128)(2,1)S(1)}, bf16[544,1024]{1,0:T(8,128)(2,1)S(1)}, u32[]{:S(2)}, u32[]{:S(2)}) collective-permute-start(bf16[544,1024]{1,0:T(8,128)(2,1)S(1)} %get-tuple-element.56.own_ref), channel_id=1, source_target_pairs={{0,8},{8,0},{16,24},{24,16},{1,9},{9,1},{17,25},{25,17},{2,10},{10... | collective-permute-start | bytes 3342344 | tf_op jit(solution)/shard_map/ppermute | solution.py:506
  7.0 2.8 %collective-permute-start.1 = (bf16[32,1024]{1,0:T(8,128)(2,1)S(1)}, bf16[32,1024]{1,0:T(8,128)(2,1)S(1)}, u32[]{:S(2)}, u32[]{:S(2)}) collective-permute-start(bf16[32,1024]{1,0:T(8,128)(2,1)S(1)} %pad_maximum_fusion), channel_id=1, source_target_pairs={{0,8},{8,0},{16,24},{24,16},{1,9},{9,1},{17,25},{25,17},{2,10},{10... | collective-permute-start | bytes 196616 | tf_op jit(solution)/shard_map/ppermute | solution.py:506
  7.5 8.9 %collective-permute-start.3 = (bf16[256,512]{1,0:T(8,128)(2,1)S(1)}, bf16[256,512]{1,0:T(8,128)(2,1)S(1)}, u32[]{:S(2)}, u32[]{:S(2)}) collective-permute-start(bf16[256,512]{1,0:T(8,128)(2,1)S(1)} %get-tuple-element.61), channel_id=1, source_target_pairs={{0,16},{8,24},{16,0},{24,8},{1,17},{9,25},{17,1},{25,9},{2,18},{10... | collective-permute-start | bytes 786440 | tf_op jit(solution)/shard_map/ppermute | solution.py:506
  12.6 10.8 %collective-permute-start.4 = (bf16[320,512]{1,0:T(8,128)(2,1)S(1)}, bf16[320,512]{1,0:T(8,128)(2,1)S(1)}, u32[]{:S(2)}, u32[]{:S(2)}) collective-permute-start(bf16[320,512]{1,0:T(8,128)(2,1)S(1)} %get-tuple-element.64), channel_id=1, source_target_pairs={{0,16},{8,24},{16,0},{24,8},{1,17},{9,25},{17,1},{25,9},{2,18},{10... | collective-permute-start | bytes 983048 | tf_op jit(solution)/shard_map/ppermute | solution.py:506
  17.7 1.3 %collective-permute-start.6 = (f32[1,128,128]{2,1,0:T(8,128)S(1)}, f32[1,128,128]{2,1,0:T(8,128)S(1)}, u32[]{:S(2)}, u32[]{:S(2)}) collective-permute-start(f32[1,128,128]{2,1,0:T(8,128)S(1)} %get-tuple-element.69), channel_id=1, source_target_pairs={{0,8},{8,0},{16,24},{24,16},{1,9},{9,1},{17,25},{25,17},{2,10},{10... | collective-permute-start | bytes 196616 | tf_op jit(solution)/shard_map/ppermute | solution.py:506
  17.7 3.0 %collective-permute-start.5 = (f32[1,128,128]{2,1,0:T(8,128)S(1)}, f32[1,128,128]{2,1,0:T(8,128)S(1)}, u32[]{:S(2)}, u32[]{:S(2)}) collective-permute-start(f32[1,128,128]{2,1,0:T(8,128)S(1)} %get-tuple-element.66), channel_id=1, source_target_pairs={{0,8},{8,0},{16,24},{24,16},{1,9},{9,1},{17,25},{25,17},{2,10},{10... | collective-permute-start | bytes 196616 | tf_op jit(solution)/shard_map/ppermute | solution.py:506
  19.0 5.5 %collective-permute-start.7 = (f32[1,128,128]{2,1,0:T(8,128)S(1)}, f32[1,128,128]{2,1,0:T(8,128)S(1)}, u32[]{:S(2)}, u32[]{:S(2)}) collective-permute-start(f32[1,128,128]{2,1,0:T(8,128)S(1)} %add.19), channel_id=1, source_target_pairs={{0,16},{8,24},{16,0},{24,8},{1,17},{9,25},{17,1},{25,9},{2,18},{10... | collective-permute-start | bytes 196616 | tf_op jit(solution)/shard_map/ppermute | solution.py:506
  24.5 2.3 %collective-permute-start.9 = (bf16[320,512]{1,0:T(8,128)(2,1)S(1)}, bf16[320,512]{1,0:T(8,128)(2,1)S(1)}, u32[]{:S(2)}, u32[]{:S(2)}) collective-permute-start(bf16[320,512]{1,0:T(8,128)(2,1)S(1)} %collective-permute-done.4.refs_12_), channel_id=1, source_target_pairs={{0,8},{8,0},{16,24},{24,16},{1,9},{9,1},{17,25},{25,17},{2,10},{10... | collective-permute-start | bytes 983048 | tf_op jit(solution)/shard_map/ppermute | solution.py:506
  24.6 2.2 %collective-permute-start.8 = (bf16[256,512]{1,0:T(8,128)(2,1)S(1)}, bf16[256,512]{1,0:T(8,128)(2,1)S(1)}, u32[]{:S(2)}, u32[]{:S(2)}) collective-permute-start(bf16[256,512]{1,0:T(8,128)(2,1)S(1)} %collective-permute-done.3.refs_0_.refs_11_), channel_id=1, source_target_pairs={{0,8},{8,0},{16,24},{24,16},{1,9},{9,1},{17,25},{25,17},{2,10},{10... | collective-permute-start | bytes 786440 | tf_op jit(solution)/shard_map/ppermute | solution.py:506
  25.1 4.3 %collective-permute-start.10 = (f32[128,128]{1,0:T(8,128)S(1)}, f32[128,128]{1,0:T(8,128)S(1)}, u32[]{:S(2)}, u32[]{:S(2)}) collective-permute-start(f32[128,128]{1,0:T(8,128)S(1)} %bitcast.1), channel_id=1, source_target_pairs={{0,1},{1,0},{2,3},{3,2},{4,5},{5,4},{6,7},{7,6},{8,9},{9,8},{10,11... | collective-permute-start | bytes 196616 | tf_op jit(solution)/shard_map/ppermute | solution.py:656
  29.4 4.9 %collective-permute-start.11 = (f32[128,128]{1,0:T(8,128)S(1)}, f32[128,128]{1,0:T(8,128)S(1)}, u32[]{:S(2)}, u32[]{:S(2)}) collective-permute-start(f32[128,128]{1,0:T(8,128)S(1)} %add.21), channel_id=1, source_target_pairs={{0,2},{1,3},{2,0},{3,1},{4,6},{5,7},{6,4},{7,5},{8,10},{9,11},{10,... | collective-permute-start | bytes 196616 | tf_op jit(solution)/shard_map/ppermute | solution.py:656
  34.3 5.2 %collective-permute-start.12 = (f32[128,128]{1,0:T(8,128)S(1)}, f32[128,128]{1,0:T(8,128)S(1)}, u32[]{:S(2)}, u32[]{:S(2)}) collective-permute-start(f32[128,128]{1,0:T(8,128)S(1)} %add.22), channel_id=1, source_target_pairs={{0,4},{1,5},{2,6},{3,7},{4,0},{5,1},{6,2},{7,3},{8,12},{9,13},{10,... | collective-permute-start | bytes 196616 | tf_op jit(solution)/shard_map/ppermute | solution.py:656
where the time goes:
time: 40.3 us; the launch traced here: 40.2 us
  starting transfers between devices  16.8 us (42%)
  Pallas kernels  13.7 us (34%)
  waiting for transfers between devices  8.26 us (20%)
  between operations  0.76 us (2%)
  other arithmetic  0.69 us (2%)
    pallas_call x8, Pallas kernels, call(): pl.pallas_call(kernel, out_shape=outs, in_specs=in_specs or [VMEM] * len(...  13.7 us
    ppermute x10, starting transfers between devices, swap(): return lax.ppermute(block, 'seq', [(i, i ^ bit) for i in range(blocks)])  10.5 us
    ppermute x10, waiting for transfers between devices, swap(): return lax.ppermute(block, 'seq', [(i, i ^ bit) for i in range(blocks)])  7.27 us
    ppermute x3, starting transfers between devices, per_device(): lax.ppermute(grad_filter, 'chan', [(i, i ^ step) for i in range(chans)])  6.23 us
    ppermute x3, waiting for transfers between devices, per_device(): lax.ppermute(grad_filter, 'chan', [(i, i ^ step) for i in range(chans)])  1 us
  transfers between devices with their start and end apart: 13, of which 8 were waited for; matrix products, arithmetic and copies ran while one was open for 0% of the time, Pallas kernels for 30%

commit v1 on v0

--- a/solution.py
+++ b/solution.py
@@ -564,6 +564,7 @@
             pltpu.VMEM((blocks + 1, 3, EDGE, width), F32),
             pltpu.VMEM((2 * EDGE, width), F32),
         ],
+        cost=32 * length * width,
     )
     filter_rows = length * groups // width
     pair_shape = shape((4 * length + 2 * filter_rows, width), BF16)
@@ -586,12 +587,12 @@
             units.update(arrived)
         return [units[index] for index in range(1, chips)]
 
-    firsts = gather([after(unit, all_marks[0]) for unit in own_units[0::2]])
-    sibling = swap(after(pair, all_marks[0]), 1)
+    firsts = gather(own_units[0::2])
+    sibling = swap(pair, 1)
     spec, near = call(
         functools.partial(chip_kernel, tile_width, groups, margin),
         [shape((4, 2 * length, width), F32), shape((2, 2 * length, groups), F32)],
-        [pair, sibling, firsts_true, forward],
+        [after(pair, *firsts), sibling, firsts_true, forward],
         [],
     )
     shares = call(
@@ -600,7 +601,7 @@
         [spec, near, firsts_true, forward, inverse, *firsts],
         [pltpu.VMEM((blocks + 1, 2 * length, groups), F32)],
     )
-    laters = gather([after(unit, near) for unit in own_units[1::2]])
+    laters = gather([after(unit, firsts_true) for unit in own_units[1::2]])
     share, sent = shares[0] + swap(shares[1], 1), shares[2] + swap(shares[3], 1)
     for bit in bits:
         share = after(share, *laters) + swap(sent, bit)

time: 40.3 us -> 40.4 us (level)
  waiting for transfers between devices: 8.26 us -> 12 us
  starting transfers between devices: 16.8 us -> 13.1 us
    ppermute x10, waiting for transfers between devices: 7.27 us -> 10.8 us  [swap(): return lax.ppermute(block, 'seq', [(i, i ^ bit) for i in range(blocks)])]
    ppermute x10, starting transfers between devices: 10.5 us -> 7.29 us  [swap(): return lax.ppermute(block, 'seq', [(i, i ^ bit) for i in range(blocks)])]
    ppermute x3, starting transfers between devices: 6.23 us -> 5.77 us  [per_device(): lax.ppermute(grad_filter, 'chan', [(i, i ^ step) for i in range(chans)])]
  transfers between devices with their start and end apart: 13 -> 13, of which waited for: 8 -> 8; matrix products, arithmetic and copies ran while one was open for 0% -> 0% of each run, Pallas kernels for 30% -> 28%
where the time goes in v1:
time: 40.4 us; the launch traced here: 40.2 us
  Pallas kernels  13.7 us (34%)
  starting transfers between devices  13.1 us (32%)
  waiting for transfers between devices  12 us (30%)
  between operations  0.76 us (2%)
  other arithmetic  0.69 us (2%)
    pallas_call x8, Pallas kernels, call(): pl.pallas_call(kernel, out_shape=outs, in_specs=in_specs or [VMEM] * len(...  13.7 us
    ppermute x10, waiting for transfers between devices, swap(): return lax.ppermute(block, 'seq', [(i, i ^ bit) for i in range(blocks)])  10.8 us
    ppermute x10, starting transfers between devices, swap(): return lax.ppermute(block, 'seq', [(i, i ^ bit) for i in range(blocks)])  7.29 us
    ppermute x3, starting transfers between devices, per_device(): lax.ppermute(grad_filter, 'chan', [(i, i ^ step) for i in range(chans)])  5.77 us
    ppermute x3, waiting for transfers between devices, per_device(): lax.ppermute(grad_filter, 'chan', [(i, i ^ step) for i in range(chans)])  1.24 us
  transfers between devices with their start and end apart: 13, of which 8 were waited for; matrix products, arithmetic and copies ran while one was open for 0% of the time, Pallas kernels for 28%

profile of v1, /device:TPU:0, one launch (start us, length us, event | category | flops | bytes accessed | tf_op | source)
XLA Modules:
  0.0 40.2 jit_solution(2181503163914411966)
XLA Ops:
  0.6 1.4 %shard_map.119 = (bf16[4,128,1024]{2,1,0:T(8,128)(2,1)S(1)}, bf16[16,1024]{1,0:T(8,128)(2,1)S(1)}, f32[3,3,1024]{2,1,0:T(4,128)S(1)}, f32[128,128]{1,0:T(8,128)S...) custom-call(bf16[128,1024]{1,0:T(8,128)(2,1)} %q_hbm.1, bf16[128,1024]{1,0:T(8,128)(2,1)} %k_hbm.1, ...), custom_call_target="tpu_custom_call" | custom-call | flops 1 | bytes 1 | tf_op jit(solution)/shard_map/pallas_call | solution.py:510
  2.1 1.1 %shard_map.120 = (bf16[544,1024]{1,0:T(8,128)(2,1)S(1)}, f32[3,128,1024]{2,1,0:T(8,128)S(1)}, bf16[256,512]{1,0:T(8,128)(2,1)S(1)}, bf16[320,512]{1,0:T(8,128)(2,1)S(1)}) custom-call(bf16[4,128,1024]{2,1,0:T(8,128)(2,1)S(1)} %get-tuple-element.46.rows_ref.refs_0_, f32[3,3,1024]{2,1,0:T(4,128)S(1)} %get-tuple-element.47.taps_ref.refs_1_, ...), custom_call_target="tpu_custom_call" | custom-call | flops 1 | bytes 5242880 | tf_op jit(solution)/shard_map/pallas_call | solution.py:510
  3.2 0.5 %collective-permute-start.2 = (bf16[544,1024]{1,0:T(8,128)(2,1)S(1)}, bf16[544,1024]{1,0:T(8,128)(2,1)S(1)}, u32[]{:S(2)}, u32[]{:S(2)}) collective-permute-start(bf16[544,1024]{1,0:T(8,128)(2,1)S(1)} %get-tuple-element.56.own_ref), channel_id=1, source_target_pairs={{0,8},{8,0},{16,24},{24,16},{1,9},{9,1},{17,25},{25,17},{2,10},{10... | collective-permute-start | bytes 3342344 | tf_op jit(solution)/shard_map/ppermute | solution.py:506
  3.7 2.6 %collective-permute-start = (bf16[16,1024]{1,0:T(8,128)(2,1)S(1)}, bf16[16,1024]{1,0:T(8,128)(2,1)S(1)}, u32[]{:S(2)}, u32[]{:S(2)}) collective-permute-start(bf16[16,1024]{1,0:T(8,128)(2,1)S(1)} %get-tuple-element.50.own_marks), channel_id=1, source_target_pairs={{0,16},{8,24},{16,0},{24,8},{1,17},{9,25},{17,1},{25,9},{2,18},{10... | collective-permute-start | bytes 98312 | tf_op jit(solution)/shard_map/ppermute | solution.py:506
  6.4 1.9 %collective-permute-done.refs_0_ = bf16[16,1024]{1,0:T(8,128)(2,1)S(1)} collective-permute-done((bf16[16,1024]{1,0:T(8,128)(2,1)S(1)}, bf16[16,1024]{1,0:T(8,128)(2,1)S(1)}, u32[]{:S(2)}, u32[]{:S(2)}) %collective-permute-start) | collective-permute-done | bytes 32800 | tf_op jit(solution)/shard_map/ppermute | solution.py:506
  8.3 1.2 %collective-permute-done.1.refs_1_ = bf16[32,1024]{1,0:T(8,128)(2,1)S(1)} collective-permute-done((bf16[32,1024]{1,0:T(8,128)(2,1)S(1)}, bf16[32,1024]{1,0:T(8,128)(2,1)S(1)}, u32[]{:S(2)}, u32[]{:S(2)}) %collective-permute-start.1) | collective-permute-done | bytes 65568 | tf_op jit(solution)/shard_map/ppermute | solution.py:506
  9.9 2.3 %collective-permute-start.4 = (bf16[320,512]{1,0:T(8,128)(2,1)S(1)}, bf16[320,512]{1,0:T(8,128)(2,1)S(1)}, u32[]{:S(2)}, u32[]{:S(2)}) collective-permute-start(bf16[320,512]{1,0:T(8,128)(2,1)S(1)} %get-tuple-element.61), channel_id=1, source_target_pairs={{0,16},{8,24},{16,0},{24,8},{1,17},{9,25},{17,1},{25,9},{2,18},{10... | collective-permute-start | bytes 983048 | tf_op jit(solution)/shard_map/ppermute | solution.py:506
  12.2 3.3 %collective-permute-done.3.refs_0_.refs_11_ = bf16[256,512]{1,0:T(8,128)(2,1)S(1)} collective-permute-done((bf16[256,512]{1,0:T(8,128)(2,1)S(1)}, bf16[256,512]{1,0:T(8,128)(2,1)S(1)}, u32[]{:S(2)}, u32[]{:S(2)}) %collective-permute-start.3) | collective-permute-done | bytes 262176 | tf_op jit(solution)/shard_map/ppermute | solution.py:506
  15.4 2.4 %shard_map.122 = (f32[4,256,1024]{2,1,0:T(8,128)S(1)}, f32[2,256,128]{2,1,0:T(8,128)S(1)}) custom-call(bf16[544,1024]{1,0:T(8,128)(2,1)S(1)} %get-tuple-element.56.own_ref, bf16[544,1024]{1,0:T(8,128)(2,1)S(1)} %collective-permute-done.2.other_ref.refs_7_, f32[4,2,8,1024]{3,2,1,0:T(8,128)S(1)} %get-tuple-element.52.firsts_ref.refs_5_, ...), custom_call_target="tpu_custom_call" | custom-call | flops 1 | bytes 1 | tf_op jit(solution)/shard_map/pallas_call | solution.py:510
  17.8 1.3 %shard_map.123 = (f32[1,128,128]{2,1,0:T(8,128)S(1)}, f32[1,128,128]{2,1,0:T(8,128)S(1)}, f32[1,128,128]{2,1,0:T(8,128)S(1)}, f32[1,128,128]{2,1,0:T(8,128)S(1)}) custom-call(f32[4,256,1024]{2,1,0:T(8,128)S(1)} %get-tuple-element.58.spec_ref.refs_8_, f32[2,256,128]{2,1,0:T(8,128)S(1)} %get-tuple-element.62.near_ref, ...), custom_call_target="tpu_custom_call" | custom-call | flops 1 | bytes 1 | tf_op jit(solution)/shard_map/pallas_call | solution.py:510
  19.2 0.5 %collective-permute-start.5 = (f32[1,128,128]{2,1,0:T(8,128)S(1)}, f32[1,128,128]{2,1,0:T(8,128)S(1)}, u32[]{:S(2)}, u32[]{:S(2)}) collective-permute-start(f32[1,128,128]{2,1,0:T(8,128)S(1)} %get-tuple-element.64), channel_id=1, source_target_pairs={{0,8},{8,0},{16,24},{24,16},{1,9},{9,1},{17,25},{25,17},{2,10},{10... | collective-permute-start | bytes 196616 | tf_op jit(solution)/shard_map/ppermute | solution.py:506
  19.7 0.7 %collective-permute-done.6 = f32[1,128,128]{2,1,0:T(8,128)S(1)} collective-permute-done((f32[1,128,128]{2,1,0:T(8,128)S(1)}, f32[1,128,128]{2,1,0:T(8,128)S(1)}, u32[]{:S(2)}, u32[]{:S(2)}) %collective-permute-start.6) | collective-permute-done | bytes 65568 | tf_op jit(solution)/shard_map/ppermute | solution.py:506
  20.4 0.7 %collective-permute-start.7 = (f32[1,128,128]{2,1,0:T(8,128)S(1)}, f32[1,128,128]{2,1,0:T(8,128)S(1)}, u32[]{:S(2)}, u32[]{:S(2)}) collective-permute-start(f32[1,128,128]{2,1,0:T(8,128)S(1)} %add.19), channel_id=1, source_target_pairs={{0,16},{8,24},{16,0},{24,8},{1,17},{9,25},{17,1},{25,9},{2,18},{10... | collective-permute-start | bytes 196616 | tf_op jit(solution)/shard_map/ppermute | solution.py:506
  21.1 0.6 %collective-permute-done.4.refs_12_ = bf16[320,512]{1,0:T(8,128)(2,1)S(1)} collective-permute-done((bf16[320,512]{1,0:T(8,128)(2,1)S(1)}, bf16[320,512]{1,0:T(8,128)(2,1)S(1)}, u32[]{:S(2)}, u32[]{:S(2)}) %collective-permute-start.4) | collective-permute-done | bytes 327712 | tf_op jit(solution)/shard_map/ppermute | solution.py:506
  21.7 3.1 %collective-permute-done.7 = f32[1,128,128]{2,1,0:T(8,128)S(1)} collective-permute-done((f32[1,128,128]{2,1,0:T(8,128)S(1)}, f32[1,128,128]{2,1,0:T(8,128)S(1)}, u32[]{:S(2)}, u32[]{:S(2)}) %collective-permute-start.7) | collective-permute-done | bytes 65568 | tf_op jit(solution)/shard_map/ppermute | solution.py:506
  25.3 1.5 %collective-permute-start.10 = (f32[128,128]{1,0:T(8,128)S(1)}, f32[128,128]{1,0:T(8,128)S(1)}, u32[]{:S(2)}, u32[]{:S(2)}) collective-permute-start(f32[128,128]{1,0:T(8,128)S(1)} %bitcast.1), channel_id=1, source_target_pairs={{0,1},{1,0},{2,3},{3,2},{4,5},{5,4},{6,7},{7,6},{8,9},{9,8},{10,11... | collective-permute-start | bytes 196616 | tf_op jit(solution)/shard_map/ppermute | solution.py:657
  26.8 2.2 %shard_map.124 = (bf16[128,1024]{1,0:T(8,128)(2,1)}, bf16[128,1024]{1,0:T(8,128)(2,1)}, bf16[128,1024]{1,0:T(8,128)(2,1)}, bf16[128,1024]{1,0:T(8,128)(2,1)}, f3...) custom-call(bf16[4,128,1024]{2,1,0:T(8,128)(2,1)S(1)} %get-tuple-element.46.rows_ref.refs_0_, ...), custom_call_target="tpu_custom_call" | custom-call | flops 1 | bytes 2621440 | tf_op jit(solution)/shard_map/pallas_call | solution.py:510
  29.1 0.6 %collective-permute-done.10 = f32[128,128]{1,0:T(8,128)S(1)} collective-permute-done((f32[128,128]{1,0:T(8,128)S(1)}, f32[128,128]{1,0:T(8,128)S(1)}, u32[]{:S(2)}, u32[]{:S(2)}) %collective-permute-start.10) | collective-permute-done | bytes 65568 | tf_op jit(solution)/shard_map/ppermute | solution.py:657
  29.6 1.6 %collective-permute-start.11 = (f32[128,128]{1,0:T(8,128)S(1)}, f32[128,128]{1,0:T(8,128)S(1)}, u32[]{:S(2)}, u32[]{:S(2)}) collective-permute-start(f32[128,128]{1,0:T(8,128)S(1)} %add.21), channel_id=1, source_target_pairs={{0,2},{1,3},{2,0},{3,1},{4,6},{5,7},{6,4},{7,5},{8,10},{9,11},{10,... | collective-permute-start | bytes 196616 | tf_op jit(solution)/shard_map/ppermute | solution.py:657
  31.3 3.0 %shard_map.125 = (bf16[128,1024]{1,0:T(8,128)(2,1)}, bf16[128,1024]{1,0:T(8,128)(2,1)}, bf16[128,1024]{1,0:T(8,128)(2,1)}, bf16[128,1024]{1,0:T(8,128)(2,1)}) custom-call(bf16[4,128,1024]{2,1,0:T(8,128)(2,1)S(1)} %get-tuple-element.46.rows_ref.refs_0_, ...), custom_call_target="tpu_custom_call", output_to_operand_aliasing={{0}: (17, {}), {1}: (18, {}), {2}: (19, {}), {3}: (20, {})} | custom-call | flops 1 | bytes 5242880 | tf_op jit(solution)/shard_map/pallas_call | solution.py:510
  34.3 2.6 %collective-permute-start.12 = (f32[128,128]{1,0:T(8,128)S(1)}, f32[128,128]{1,0:T(8,128)S(1)}, u32[]{:S(2)}, u32[]{:S(2)}) collective-permute-start(f32[128,128]{1,0:T(8,128)S(1)} %add.22), channel_id=1, source_target_pairs={{0,4},{1,5},{2,6},{3,7},{4,0},{5,1},{6,2},{7,3},{8,12},{9,13},{10,... | collective-permute-start | bytes 196616 | tf_op jit(solution)/shard_map/ppermute | solution.py:657
  37.0 1.9 %shard_map.126 = (bf16[128,1024]{1,0:T(8,128)(2,1)}, bf16[128,1024]{1,0:T(8,128)(2,1)}, bf16[128,1024]{1,0:T(8,128)(2,1)}, bf16[128,1024]{1,0:T(8,128)(2,1)}) custom-call(bf16[4,128,1024]{2,1,0:T(8,128)(2,1)S(1)} %get-tuple-element.46.rows_ref.refs_0_, ...), custom_call_target="tpu_custom_call", output_to_operand_aliasing={{0}: (17, {}), {1}: (18, {}), {2}: (19, {}), {3}: (20, {})} | custom-call | flops 1 | bytes 2621440 | tf_op jit(solution)/shard_map/pallas_call | solution.py:510
  38.9 0.7 %collective-permute-done.12 = f32[128,128]{1,0:T(8,128)S(1)} collective-permute-done((f32[128,128]{1,0:T(8,128)S(1)}, f32[128,128]{1,0:T(8,128)S(1)}, u32[]{:S(2)}, u32[]{:S(2)}) %collective-permute-start.12) | collective-permute-done | bytes 65568 | tf_op jit(solution)/shard_map/ppermute | solution.py:657
  39.6 0.6 %add.23 = f32[128,128]{1,0:T(8,128)} add(f32[128,128]{1,0:T(8,128)S(1)} %add.22, f32[128,128]{1,0:T(8,128)S(1)} %collective-permute-done.12) | non-fusion elementwise | flops 16384 | bytes 196608 | tf_op jit(solution)/shard_map/add | solution.py:661
  (17 shorter events, 1.2 us)
Async XLA Ops:
  3.2 12.3 %collective-permute-start.2 = (bf16[544,1024]{1,0:T(8,128)(2,1)S(1)}, bf16[544,1024]{1,0:T(8,128)(2,1)S(1)}, u32[]{:S(2)}, u32[]{:S(2)}) collective-permute-start(bf16[544,1024]{1,0:T(8,128)(2,1)S(1)} %get-tuple-element.56.own_ref), channel_id=1, source_target_pairs={{0,8},{8,0},{16,24},{24,16},{1,9},{9,1},{17,25},{25,17},{2,10},{10... | collective-permute-start | bytes 3342344 | tf_op jit(solution)/shard_map/ppermute | solution.py:506
  3.7 4.6 %collective-permute-start = (bf16[16,1024]{1,0:T(8,128)(2,1)S(1)}, bf16[16,1024]{1,0:T(8,128)(2,1)S(1)}, u32[]{:S(2)}, u32[]{:S(2)}) collective-permute-start(bf16[16,1024]{1,0:T(8,128)(2,1)S(1)} %get-tuple-element.50.own_marks), channel_id=1, source_target_pairs={{0,16},{8,24},{16,0},{24,8},{1,17},{9,25},{17,1},{25,9},{2,18},{10... | collective-permute-start | bytes 98312 | tf_op jit(solution)/shard_map/ppermute | solution.py:506
  6.3 9.2 %collective-permute-start.3 = (bf16[256,512]{1,0:T(8,128)(2,1)S(1)}, bf16[256,512]{1,0:T(8,128)(2,1)S(1)}, u32[]{:S(2)}, u32[]{:S(2)}) collective-permute-start(bf16[256,512]{1,0:T(8,128)(2,1)S(1)} %get-tuple-element.55), channel_id=1, source_target_pairs={{0,16},{8,24},{16,0},{24,8},{1,17},{9,25},{17,1},{25,9},{2,18},{10... | collective-permute-start | bytes 786440 | tf_op jit(solution)/shard_map/ppermute | solution.py:506
  8.3 1.3 %collective-permute-start.1 = (bf16[32,1024]{1,0:T(8,128)(2,1)S(1)}, bf16[32,1024]{1,0:T(8,128)(2,1)S(1)}, u32[]{:S(2)}, u32[]{:S(2)}) collective-permute-start(bf16[32,1024]{1,0:T(8,128)(2,1)S(1)} %pad_maximum_fusion), channel_id=1, source_target_pairs={{0,8},{8,0},{16,24},{24,16},{1,9},{9,1},{17,25},{25,17},{2,10},{10... | collective-permute-start | bytes 196616 | tf_op jit(solution)/shard_map/ppermute | solution.py:506
  9.9 11.8 %collective-permute-start.4 = (bf16[320,512]{1,0:T(8,128)(2,1)S(1)}, bf16[320,512]{1,0:T(8,128)(2,1)S(1)}, u32[]{:S(2)}, u32[]{:S(2)}) collective-permute-start(bf16[320,512]{1,0:T(8,128)(2,1)S(1)} %get-tuple-element.61), channel_id=1, source_target_pairs={{0,16},{8,24},{16,0},{24,8},{1,17},{9,25},{17,1},{25,9},{2,18},{10... | collective-permute-start | bytes 983048 | tf_op jit(solution)/shard_map/ppermute | solution.py:506
  19.1 1.3 %collective-permute-start.6 = (f32[1,128,128]{2,1,0:T(8,128)S(1)}, f32[1,128,128]{2,1,0:T(8,128)S(1)}, u32[]{:S(2)}, u32[]{:S(2)}) collective-permute-start(f32[1,128,128]{2,1,0:T(8,128)S(1)} %get-tuple-element.67), channel_id=1, source_target_pairs={{0,8},{8,0},{16,24},{24,16},{1,9},{9,1},{17,25},{25,17},{2,10},{10... | collective-permute-start | bytes 196616 | tf_op jit(solution)/shard_map/ppermute | solution.py:506
  19.2 1.9 %collective-permute-start.5 = (f32[1,128,128]{2,1,0:T(8,128)S(1)}, f32[1,128,128]{2,1,0:T(8,128)S(1)}, u32[]{:S(2)}, u32[]{:S(2)}) collective-permute-start(f32[1,128,128]{2,1,0:T(8,128)S(1)} %get-tuple-element.64), channel_id=1, source_target_pairs={{0,8},{8,0},{16,24},{24,16},{1,9},{9,1},{17,25},{25,17},{2,10},{10... | collective-permute-start | bytes 196616 | tf_op jit(solution)/shard_map/ppermute | solution.py:506
  20.4 4.3 %collective-permute-start.7 = (f32[1,128,128]{2,1,0:T(8,128)S(1)}, f32[1,128,128]{2,1,0:T(8,128)S(1)}, u32[]{:S(2)}, u32[]{:S(2)}) collective-permute-start(f32[1,128,128]{2,1,0:T(8,128)S(1)} %add.19), channel_id=1, source_target_pairs={{0,16},{8,24},{16,0},{24,8},{1,17},{9,25},{17,1},{25,9},{2,18},{10... | collective-permute-start | bytes 196616 | tf_op jit(solution)/shard_map/ppermute | solution.py:506
  24.8 2.1 %collective-permute-start.9 = (bf16[320,512]{1,0:T(8,128)(2,1)S(1)}, bf16[320,512]{1,0:T(8,128)(2,1)S(1)}, u32[]{:S(2)}, u32[]{:S(2)}) collective-permute-start(bf16[320,512]{1,0:T(8,128)(2,1)S(1)} %collective-permute-done.4.refs_12_), channel_id=1, source_target_pairs={{0,8},{8,0},{16,24},{24,16},{1,9},{9,1},{17,25},{25,17},{2,10},{10... | collective-permute-start | bytes 983048 | tf_op jit(solution)/shard_map/ppermute | solution.py:506
  24.8 2.0 %collective-permute-start.8 = (bf16[256,512]{1,0:T(8,128)(2,1)S(1)}, bf16[256,512]{1,0:T(8,128)(2,1)S(1)}, u32[]{:S(2)}, u32[]{:S(2)}) collective-permute-start(bf16[256,512]{1,0:T(8,128)(2,1)S(1)} %collective-permute-done.3.refs_0_.refs_11_), channel_id=1, source_target_pairs={{0,8},{8,0},{16,24},{24,16},{1,9},{9,1},{17,25},{25,17},{2,10},{10... | collective-permute-start | bytes 786440 | tf_op jit(solution)/shard_map/ppermute | solution.py:506
  25.3 4.3 %collective-permute-start.10 = (f32[128,128]{1,0:T(8,128)S(1)}, f32[128,128]{1,0:T(8,128)S(1)}, u32[]{:S(2)}, u32[]{:S(2)}) collective-permute-start(f32[128,128]{1,0:T(8,128)S(1)} %bitcast.1), channel_id=1, source_target_pairs={{0,1},{1,0},{2,3},{3,2},{4,5},{5,4},{6,7},{7,6},{8,9},{9,8},{10,11... | collective-permute-start | bytes 196616 | tf_op jit(solution)/shard_map/ppermute | solution.py:657
  29.6 4.7 %collective-permute-start.11 = (f32[128,128]{1,0:T(8,128)S(1)}, f32[128,128]{1,0:T(8,128)S(1)}, u32[]{:S(2)}, u32[]{:S(2)}) collective-permute-start(f32[128,128]{1,0:T(8,128)S(1)} %add.21), channel_id=1, source_target_pairs={{0,2},{1,3},{2,0},{3,1},{4,6},{5,7},{6,4},{7,5},{8,10},{9,11},{10,... | collective-permute-start | bytes 196616 | tf_op jit(solution)/shard_map/ppermute | solution.py:657
  34.3 5.2 %collective-permute-start.12 = (f32[128,128]{1,0:T(8,128)S(1)}, f32[128,128]{1,0:T(8,128)S(1)}, u32[]{:S(2)}, u32[]{:S(2)}) collective-permute-start(f32[128,128]{1,0:T(8,128)S(1)} %add.22), channel_id=1, source_target_pairs={{0,4},{1,5},{2,6},{3,7},{4,0},{5,1},{6,2},{7,3},{8,12},{9,13},{10,... | collective-permute-start | bytes 196616 | tf_op jit(solution)/shard_map/ppermute | solution.py:657

commit v2 on v1

--- a/solution.py
+++ b/solution.py
@@ -255,13 +255,29 @@
     lax.fori_loop(0, width // tile_width, one_tile, 0)
 
 
+def unit_kernel(tile_width, margin, firsts_ref, forward_ref, *refs):
+    others = len(refs) // 2
+    length = forward_ref.shape[1] // 3
+    half = refs[0].shape[1]
+    me = lax.axis_index("seq")
+    core, chip = me % 2, me // 2
+    forward = forward_ref[0 : 2 * length]
+    for index, (unit, spec_ref) in enumerate(zip(refs[:others], refs[others:])):
+        other = chip ^ (index + 1)
+        kind = jnp.where(other < chip, 0, 1)
+        for tile in range(half // tile_width):
+            start = tile * tile_width
+            lanes = slice(start, start + tile_width)
+            wide_lanes = pl.ds(pl.multiple_of(kind * half + start, tile_width), tile_width)
+            first = firsts_ref[2 * other + core, kind, :, wide_lanes]
+            spec_ref[:, lanes] = spectrum(forward, margin, first, unit, 0, lanes)
+
+
 def filter_grad_kernel(
     blocks,
     tile_width,
-    margin,
     spec_ref,
     near_ref,
-    firsts_ref,
     forward_ref,
     inverse_ref,
     *refs,
@@ -274,7 +290,6 @@
     half = spec_ref.shape[2] // 2
     me = lax.axis_index("seq")
     core, chip = me % 2, me // 2
-    forward = forward_ref[0 : 2 * length]
     cross[0:2] = near_ref[...]
     cross[2:] = jnp.zeros((blocks - 1, 2 * length, groups), F32)
     for index, unit in enumerate(units):
@@ -285,8 +300,7 @@
             lanes = pl.ds(start, tile_width)
             kind = jnp.where(other < chip, 0, 1)
             wide_lanes = pl.ds(pl.multiple_of(kind * half + start, tile_width), tile_width)
-            first = firsts_ref[2 * other + core, kind, :, wide_lanes]
-            spec = spectrum(forward, margin, first, unit, 0, lanes)
+            spec = unit[:, lanes]
 
             @pl.when(other < chip)
             def _():
@@ -592,13 +606,20 @@
     spec, near = call(
         functools.partial(chip_kernel, tile_width, groups, margin),
         [shape((4, 2 * length, width), F32), shape((2, 2 * length, groups), F32)],
-        [after(pair, *firsts), sibling, firsts_true, forward],
+        [pair, sibling, firsts_true, forward],
         [],
     )
+    unit_specs = call(
+        functools.partial(unit_kernel, tile_width, margin),
+        [shape((2 * length, half), F32)] * (chips - 1),
+        [after(firsts_true, near), forward, *firsts],
+        [],
+        cost=80 * length * width,
+    )
     shares = call(
-        functools.partial(filter_grad_kernel, blocks, tile_width, margin),
+        functools.partial(filter_grad_kernel, blocks, tile_width),
         [shape((blocks // 4, length, groups), F32)] * 4,
-        [spec, near, firsts_true, forward, inverse, *firsts],
+        [spec, near, forward, inverse, *unit_specs],
         [pltpu.VMEM((blocks + 1, 2 * length, groups), F32)],
     )
     laters = gather([after(unit, firsts_true) for unit in own_units[1::2]])

time: 40.4 us -> 38.7 us (0.958)
  waiting for transfers between devices: 12 us -> 10.5 us
    ppermute x10, waiting for transfers between devices: 10.8 us -> 9.22 us  [swap(): return lax.ppermute(block, 'seq', [(i, i ^ bit) for i in range(blocks)])]
    pallas_call x8 -> x9, Pallas kernels: 13.7 us -> 13.5 us  [call(): pl.pallas_call(kernel, out_shape=outs, in_specs=in_specs or [VMEM] * len(...]
  transfers between devices with their start and end apart: 13 -> 13, of which waited for: 8 -> 8; matrix products, arithmetic and copies ran while one was open for 0% -> 0% of each run, Pallas kernels for 28% -> 29%
where the time goes in v2:
time: 38.7 us; the launch traced here: 38.5 us
  Pallas kernels  13.5 us (35%)
  starting transfers between devices  13.1 us (34%)
  waiting for transfers between devices  10.5 us (27%)
  between operations  0.76 us (2%)
  other arithmetic  0.69 us (2%)
    pallas_call x9, Pallas kernels, call(): pl.pallas_call(kernel, out_shape=outs, in_specs=in_specs or [VMEM] * len(...  13.5 us
    ppermute x10, waiting for transfers between devices, swap(): return lax.ppermute(block, 'seq', [(i, i ^ bit) for i in range(blocks)])  9.22 us
    ppermute x10, starting transfers between devices, swap(): return lax.ppermute(block, 'seq', [(i, i ^ bit) for i in range(blocks)])  7.3 us
    ppermute x3, starting transfers between devices, per_device(): lax.ppermute(grad_filter, 'chan', [(i, i ^ step) for i in range(chans)])  5.79 us
    ppermute x3, waiting for transfers between devices, per_device(): lax.ppermute(grad_filter, 'chan', [(i, i ^ step) for i in range(chans)])  1.24 us
  transfers between devices with their start and end apart: 13, of which 8 were waited for; matrix products, arithmetic and copies ran while one was open for 0% of the time, Pallas kernels for 29%

profile of v2, /device:TPU:0, one launch (start us, length us, event | category | flops | bytes accessed | tf_op | source)
XLA Modules:
  0.0 38.5 jit_solution(17732993802402228085)
XLA Ops:
  0.6 1.4 %shard_map.119 = (bf16[4,128,1024]{2,1,0:T(8,128)(2,1)S(1)}, bf16[16,1024]{1,0:T(8,128)(2,1)S(1)}, f32[3,3,1024]{2,1,0:T(4,128)S(1)}, f32[128,128]{1,0:T(8,128)S...) custom-call(bf16[128,1024]{1,0:T(8,128)(2,1)} %q_hbm.1, bf16[128,1024]{1,0:T(8,128)(2,1)} %k_hbm.1, ...), custom_call_target="tpu_custom_call" | custom-call | flops 1 | bytes 1 | tf_op jit(solution)/shard_map/pallas_call | solution.py:524
  2.1 1.1 %shard_map.120 = (bf16[544,1024]{1,0:T(8,128)(2,1)S(1)}, f32[3,128,1024]{2,1,0:T(8,128)S(1)}, bf16[256,512]{1,0:T(8,128)(2,1)S(1)}, bf16[320,512]{1,0:T(8,128)(2,1)S(1)}) custom-call(bf16[4,128,1024]{2,1,0:T(8,128)(2,1)S(1)} %get-tuple-element.46.rows_ref.refs_0_, f32[3,3,1024]{2,1,0:T(4,128)S(1)} %get-tuple-element.47.taps_ref.refs_1_, ...), custom_call_target="tpu_custom_call" | custom-call | flops 1 | bytes 5242880 | tf_op jit(solution)/shard_map/pallas_call | solution.py:524
  3.2 0.5 %collective-permute-start.2 = (bf16[544,1024]{1,0:T(8,128)(2,1)S(1)}, bf16[544,1024]{1,0:T(8,128)(2,1)S(1)}, u32[]{:S(2)}, u32[]{:S(2)}) collective-permute-start(bf16[544,1024]{1,0:T(8,128)(2,1)S(1)} %get-tuple-element.54.own_ref), channel_id=1, source_target_pairs={{0,8},{8,0},{16,24},{24,16},{1,9},{9,1},{17,25},{25,17},{2,10},{10... | collective-permute-start | bytes 3342344 | tf_op jit(solution)/shard_map/ppermute | solution.py:520
  3.7 2.6 %collective-permute-start = (bf16[16,1024]{1,0:T(8,128)(2,1)S(1)}, bf16[16,1024]{1,0:T(8,128)(2,1)S(1)}, u32[]{:S(2)}, u32[]{:S(2)}) collective-permute-start(bf16[16,1024]{1,0:T(8,128)(2,1)S(1)} %get-tuple-element.50.own_marks), channel_id=1, source_target_pairs={{0,16},{8,24},{16,0},{24,8},{1,17},{9,25},{17,1},{25,9},{2,18},{10... | collective-permute-start | bytes 98312 | tf_op jit(solution)/shard_map/ppermute | solution.py:520
  6.4 1.9 %collective-permute-done.refs_0_ = bf16[16,1024]{1,0:T(8,128)(2,1)S(1)} collective-permute-done((bf16[16,1024]{1,0:T(8,128)(2,1)S(1)}, bf16[16,1024]{1,0:T(8,128)(2,1)S(1)}, u32[]{:S(2)}, u32[]{:S(2)}) %collective-permute-start) | collective-permute-done | bytes 32800 | tf_op jit(solution)/shard_map/ppermute | solution.py:520
  8.3 1.2 %collective-permute-done.1.refs_1_ = bf16[32,1024]{1,0:T(8,128)(2,1)S(1)} collective-permute-done((bf16[32,1024]{1,0:T(8,128)(2,1)S(1)}, bf16[32,1024]{1,0:T(8,128)(2,1)S(1)}, u32[]{:S(2)}, u32[]{:S(2)}) %collective-permute-start.1) | collective-permute-done | bytes 65568 | tf_op jit(solution)/shard_map/ppermute | solution.py:520
  9.9 2.3 %collective-permute-start.4 = (bf16[320,512]{1,0:T(8,128)(2,1)S(1)}, bf16[320,512]{1,0:T(8,128)(2,1)S(1)}, u32[]{:S(2)}, u32[]{:S(2)}) collective-permute-start(bf16[320,512]{1,0:T(8,128)(2,1)S(1)} %get-tuple-element.60), channel_id=1, source_target_pairs={{0,16},{8,24},{16,0},{24,8},{1,17},{9,25},{17,1},{25,9},{2,18},{10... | collective-permute-start | bytes 983048 | tf_op jit(solution)/shard_map/ppermute | solution.py:520
  12.2 2.4 %shard_map.122 = (f32[4,256,1024]{2,1,0:T(8,128)S(1)}, f32[2,256,128]{2,1,0:T(8,128)S(1)}) custom-call(bf16[544,1024]{1,0:T(8,128)(2,1)S(1)} %get-tuple-element.54.own_ref, bf16[544,1024]{1,0:T(8,128)(2,1)S(1)} %collective-permute-done.2.other_ref.refs_7_, f32[4,2,8,1024]{3,2,1,0:T(8,128)S(1)} %get-tuple-element.62.firsts_ref.refs_5_, ...), custom_call_target="tpu_custom_call" | custom-call | flops 1 | bytes 1 | tf_op jit(solution)/shard_map/pallas_call | solution.py:524
  14.6 0.9 %collective-permute-done.3.refs_0_.refs_11_ = bf16[256,512]{1,0:T(8,128)(2,1)S(1)} collective-permute-done((bf16[256,512]{1,0:T(8,128)(2,1)S(1)}, bf16[256,512]{1,0:T(8,128)(2,1)S(1)}, u32[]{:S(2)}, u32[]{:S(2)}) %collective-permute-start.3) | collective-permute-done | bytes 262176 | tf_op jit(solution)/shard_map/ppermute | solution.py:520
  15.8 0.8 %shard_map.124 = (f32[1,128,128]{2,1,0:T(8,128)S(1)}, f32[1,128,128]{2,1,0:T(8,128)S(1)}, f32[1,128,128]{2,1,0:T(8,128)S(1)}, f32[1,128,128]{2,1,0:T(8,128)S(1)}) custom-call(f32[4,256,1024]{2,1,0:T(8,128)S(1)} %get-tuple-element.56.spec_ref.refs_8_, f32[2,256,128]{2,1,0:T(8,128)S(1)} %get-tuple-element.61.near_ref, ...), custom_call_target="tpu_custom_call" | custom-call | flops 1 | bytes 1 | tf_op jit(solution)/shard_map/pallas_call | solution.py:524
  16.7 0.5 %collective-permute-start.5 = (f32[1,128,128]{2,1,0:T(8,128)S(1)}, f32[1,128,128]{2,1,0:T(8,128)S(1)}, u32[]{:S(2)}, u32[]{:S(2)}) collective-permute-start(f32[1,128,128]{2,1,0:T(8,128)S(1)} %get-tuple-element.64), channel_id=1, source_target_pairs={{0,8},{8,0},{16,24},{24,16},{1,9},{9,1},{17,25},{25,17},{2,10},{10... | collective-permute-start | bytes 196616 | tf_op jit(solution)/shard_map/ppermute | solution.py:520
  17.2 0.7 %collective-permute-done.6 = f32[1,128,128]{2,1,0:T(8,128)S(1)} collective-permute-done((f32[1,128,128]{2,1,0:T(8,128)S(1)}, f32[1,128,128]{2,1,0:T(8,128)S(1)}, u32[]{:S(2)}, u32[]{:S(2)}) %collective-permute-start.6) | collective-permute-done | bytes 65568 | tf_op jit(solution)/shard_map/ppermute | solution.py:520
  17.9 0.7 %collective-permute-start.7 = (f32[1,128,128]{2,1,0:T(8,128)S(1)}, f32[1,128,128]{2,1,0:T(8,128)S(1)}, u32[]{:S(2)}, u32[]{:S(2)}) collective-permute-start(f32[1,128,128]{2,1,0:T(8,128)S(1)} %add.19), channel_id=1, source_target_pairs={{0,16},{8,24},{16,0},{24,8},{1,17},{9,25},{17,1},{25,9},{2,18},{10... | collective-permute-start | bytes 196616 | tf_op jit(solution)/shard_map/ppermute | solution.py:520
  18.6 3.7 %collective-permute-done.4.refs_12_ = bf16[320,512]{1,0:T(8,128)(2,1)S(1)} collective-permute-done((bf16[320,512]{1,0:T(8,128)(2,1)S(1)}, bf16[320,512]{1,0:T(8,128)(2,1)S(1)}, u32[]{:S(2)}, u32[]{:S(2)}) %collective-permute-start.4) | collective-permute-done | bytes 327712 | tf_op jit(solution)/shard_map/ppermute | solution.py:520
  22.4 0.7 %collective-permute-done.7 = f32[1,128,128]{2,1,0:T(8,128)S(1)} collective-permute-done((f32[1,128,128]{2,1,0:T(8,128)S(1)}, f32[1,128,128]{2,1,0:T(8,128)S(1)}, u32[]{:S(2)}, u32[]{:S(2)}) %collective-permute-start.7) | collective-permute-done | bytes 65568 | tf_op jit(solution)/shard_map/ppermute | solution.py:520
  23.7 1.5 %collective-permute-start.10 = (f32[128,128]{1,0:T(8,128)S(1)}, f32[128,128]{1,0:T(8,128)S(1)}, u32[]{:S(2)}, u32[]{:S(2)}) collective-permute-start(f32[128,128]{1,0:T(8,128)S(1)} %bitcast.1), channel_id=1, source_target_pairs={{0,1},{1,0},{2,3},{3,2},{4,5},{5,4},{6,7},{7,6},{8,9},{9,8},{10,11... | collective-permute-start | bytes 196616 | tf_op jit(solution)/shard_map/ppermute | solution.py:678
  25.2 2.2 %shard_map.125 = (bf16[128,1024]{1,0:T(8,128)(2,1)}, bf16[128,1024]{1,0:T(8,128)(2,1)}, bf16[128,1024]{1,0:T(8,128)(2,1)}, bf16[128,1024]{1,0:T(8,128)(2,1)}, f3...) custom-call(bf16[4,128,1024]{2,1,0:T(8,128)(2,1)S(1)} %get-tuple-element.46.rows_ref.refs_0_, ...), custom_call_target="tpu_custom_call" | custom-call | flops 1 | bytes 2621440 | tf_op jit(solution)/shard_map/pallas_call | solution.py:524
  27.4 0.5 %collective-permute-done.10 = f32[128,128]{1,0:T(8,128)S(1)} collective-permute-done((f32[128,128]{1,0:T(8,128)S(1)}, f32[128,128]{1,0:T(8,128)S(1)}, u32[]{:S(2)}, u32[]{:S(2)}) %collective-permute-start.10) | collective-permute-done | bytes 65568 | tf_op jit(solution)/shard_map/ppermute | solution.py:678
  28.0 1.6 %collective-permute-start.11 = (f32[128,128]{1,0:T(8,128)S(1)}, f32[128,128]{1,0:T(8,128)S(1)}, u32[]{:S(2)}, u32[]{:S(2)}) collective-permute-start(f32[128,128]{1,0:T(8,128)S(1)} %add.21), channel_id=1, source_target_pairs={{0,2},{1,3},{2,0},{3,1},{4,6},{5,7},{6,4},{7,5},{8,10},{9,11},{10,... | collective-permute-start | bytes 196616 | tf_op jit(solution)/shard_map/ppermute | solution.py:678
  29.6 3.0 %shard_map.126 = (bf16[128,1024]{1,0:T(8,128)(2,1)}, bf16[128,1024]{1,0:T(8,128)(2,1)}, bf16[128,1024]{1,0:T(8,128)(2,1)}, bf16[128,1024]{1,0:T(8,128)(2,1)}) custom-call(bf16[4,128,1024]{2,1,0:T(8,128)(2,1)S(1)} %get-tuple-element.46.rows_ref.refs_0_, ...), custom_call_target="tpu_custom_call", output_to_operand_aliasing={{0}: (17, {}), {1}: (18, {}), {2}: (19, {}), {3}: (20, {})} | custom-call | flops 1 | bytes 5242880 | tf_op jit(solution)/shard_map/pallas_call | solution.py:524
  32.6 2.7 %collective-permute-start.12 = (f32[128,128]{1,0:T(8,128)S(1)}, f32[128,128]{1,0:T(8,128)S(1)}, u32[]{:S(2)}, u32[]{:S(2)}) collective-permute-start(f32[128,128]{1,0:T(8,128)S(1)} %add.22), channel_id=1, source_target_pairs={{0,4},{1,5},{2,6},{3,7},{4,0},{5,1},{6,2},{7,3},{8,12},{9,13},{10,... | collective-permute-start | bytes 196616 | tf_op jit(solution)/shard_map/ppermute | solution.py:678
  35.3 1.9 %shard_map.127 = (bf16[128,1024]{1,0:T(8,128)(2,1)}, bf16[128,1024]{1,0:T(8,128)(2,1)}, bf16[128,1024]{1,0:T(8,128)(2,1)}, bf16[128,1024]{1,0:T(8,128)(2,1)}) custom-call(bf16[4,128,1024]{2,1,0:T(8,128)(2,1)S(1)} %get-tuple-element.46.rows_ref.refs_0_, ...), custom_call_target="tpu_custom_call", output_to_operand_aliasing={{0}: (17, {}), {1}: (18, {}), {2}: (19, {}), {3}: (20, {})} | custom-call | flops 1 | bytes 2621440 | tf_op jit(solution)/shard_map/pallas_call | solution.py:524
  37.2 0.7 %collective-permute-done.12 = f32[128,128]{1,0:T(8,128)S(1)} collective-permute-done((f32[128,128]{1,0:T(8,128)S(1)}, f32[128,128]{1,0:T(8,128)S(1)}, u32[]{:S(2)}, u32[]{:S(2)}) %collective-permute-start.12) | collective-permute-done | bytes 65568 | tf_op jit(solution)/shard_map/ppermute | solution.py:678
  37.9 0.6 %add.23 = f32[128,128]{1,0:T(8,128)} add(f32[128,128]{1,0:T(8,128)S(1)} %add.22, f32[128,128]{1,0:T(8,128)S(1)} %collective-permute-done.12) | non-fusion elementwise | flops 16384 | bytes 196608 | tf_op jit(solution)/shard_map/add | solution.py:682
  (18 shorter events, 1.5 us)
Async XLA Ops:
  3.2 9.0 %collective-permute-start.2 = (bf16[544,1024]{1,0:T(8,128)(2,1)S(1)}, bf16[544,1024]{1,0:T(8,128)(2,1)S(1)}, u32[]{:S(2)}, u32[]{:S(2)}) collective-permute-start(bf16[544,1024]{1,0:T(8,128)(2,1)S(1)} %get-tuple-element.54.own_ref), channel_id=1, source_target_pairs={{0,8},{8,0},{16,24},{24,16},{1,9},{9,1},{17,25},{25,17},{2,10},{10... | collective-permute-start | bytes 3342344 | tf_op jit(solution)/shard_map/ppermute | solution.py:520
  3.7 4.6 %collective-permute-start = (bf16[16,1024]{1,0:T(8,128)(2,1)S(1)}, bf16[16,1024]{1,0:T(8,128)(2,1)S(1)}, u32[]{:S(2)}, u32[]{:S(2)}) collective-permute-start(bf16[16,1024]{1,0:T(8,128)(2,1)S(1)} %get-tuple-element.50.own_marks), channel_id=1, source_target_pairs={{0,16},{8,24},{16,0},{24,8},{1,17},{9,25},{17,1},{25,9},{2,18},{10... | collective-permute-start | bytes 98312 | tf_op jit(solution)/shard_map/ppermute | solution.py:520
  6.3 9.2 %collective-permute-start.3 = (bf16[256,512]{1,0:T(8,128)(2,1)S(1)}, bf16[256,512]{1,0:T(8,128)(2,1)S(1)}, u32[]{:S(2)}, u32[]{:S(2)}) collective-permute-start(bf16[256,512]{1,0:T(8,128)(2,1)S(1)} %get-tuple-element.58), channel_id=1, source_target_pairs={{0,16},{8,24},{16,0},{24,8},{1,17},{9,25},{17,1},{25,9},{2,18},{10... | collective-permute-start | bytes 786440 | tf_op jit(solution)/shard_map/ppermute | solution.py:520
  8.3 1.3 %collective-permute-start.1 = (bf16[32,1024]{1,0:T(8,128)(2,1)S(1)}, bf16[32,1024]{1,0:T(8,128)(2,1)S(1)}, u32[]{:S(2)}, u32[]{:S(2)}) collective-permute-start(bf16[32,1024]{1,0:T(8,128)(2,1)S(1)} %pad_maximum_fusion), channel_id=1, source_target_pairs={{0,8},{8,0},{16,24},{24,16},{1,9},{9,1},{17,25},{25,17},{2,10},{10... | collective-permute-start | bytes 196616 | tf_op jit(solution)/shard_map/ppermute | solution.py:520
  9.9 12.5 %collective-permute-start.4 = (bf16[320,512]{1,0:T(8,128)(2,1)S(1)}, bf16[320,512]{1,0:T(8,128)(2,1)S(1)}, u32[]{:S(2)}, u32[]{:S(2)}) collective-permute-start(bf16[320,512]{1,0:T(8,128)(2,1)S(1)} %get-tuple-element.60), channel_id=1, source_target_pairs={{0,16},{8,24},{16,0},{24,8},{1,17},{9,25},{17,1},{25,9},{2,18},{10... | collective-permute-start | bytes 983048 | tf_op jit(solution)/shard_map/ppermute | solution.py:520
  16.6 1.3 %collective-permute-start.6 = (f32[1,128,128]{2,1,0:T(8,128)S(1)}, f32[1,128,128]{2,1,0:T(8,128)S(1)}, u32[]{:S(2)}, u32[]{:S(2)}) collective-permute-start(f32[1,128,128]{2,1,0:T(8,128)S(1)} %get-tuple-element.67), channel_id=1, source_target_pairs={{0,8},{8,0},{16,24},{24,16},{1,9},{9,1},{17,25},{25,17},{2,10},{10... | collective-permute-start | bytes 196616 | tf_op jit(solution)/shard_map/ppermute | solution.py:520
  16.7 1.9 %collective-permute-start.5 = (f32[1,128,128]{2,1,0:T(8,128)S(1)}, f32[1,128,128]{2,1,0:T(8,128)S(1)}, u32[]{:S(2)}, u32[]{:S(2)}) collective-permute-start(f32[1,128,128]{2,1,0:T(8,128)S(1)} %get-tuple-element.64), channel_id=1, source_target_pairs={{0,8},{8,0},{16,24},{24,16},{1,9},{9,1},{17,25},{25,17},{2,10},{10... | collective-permute-start | bytes 196616 | tf_op jit(solution)/shard_map/ppermute | solution.py:520
  17.9 5.2 %collective-permute-start.7 = (f32[1,128,128]{2,1,0:T(8,128)S(1)}, f32[1,128,128]{2,1,0:T(8,128)S(1)}, u32[]{:S(2)}, u32[]{:S(2)}) collective-permute-start(f32[1,128,128]{2,1,0:T(8,128)S(1)} %add.19), channel_id=1, source_target_pairs={{0,16},{8,24},{16,0},{24,8},{1,17},{9,25},{17,1},{25,9},{2,18},{10... | collective-permute-start | bytes 196616 | tf_op jit(solution)/shard_map/ppermute | solution.py:520
  23.1 2.1 %collective-permute-start.9 = (bf16[320,512]{1,0:T(8,128)(2,1)S(1)}, bf16[320,512]{1,0:T(8,128)(2,1)S(1)}, u32[]{:S(2)}, u32[]{:S(2)}) collective-permute-start(bf16[320,512]{1,0:T(8,128)(2,1)S(1)} %collective-permute-done.4.refs_12_), channel_id=1, source_target_pairs={{0,8},{8,0},{16,24},{24,16},{1,9},{9,1},{17,25},{25,17},{2,10},{10... | collective-permute-start | bytes 983048 | tf_op jit(solution)/shard_map/ppermute | solution.py:520
  23.2 2.0 %collective-permute-start.8 = (bf16[256,512]{1,0:T(8,128)(2,1)S(1)}, bf16[256,512]{1,0:T(8,128)(2,1)S(1)}, u32[]{:S(2)}, u32[]{:S(2)}) collective-permute-start(bf16[256,512]{1,0:T(8,128)(2,1)S(1)} %collective-permute-done.3.refs_0_.refs_11_), channel_id=1, source_target_pairs={{0,8},{8,0},{16,24},{24,16},{1,9},{9,1},{17,25},{25,17},{2,10},{10... | collective-permute-start | bytes 786440 | tf_op jit(solution)/shard_map/ppermute | solution.py:520
  23.7 4.3 %collective-permute-start.10 = (f32[128,128]{1,0:T(8,128)S(1)}, f32[128,128]{1,0:T(8,128)S(1)}, u32[]{:S(2)}, u32[]{:S(2)}) collective-permute-start(f32[128,128]{1,0:T(8,128)S(1)} %bitcast.1), channel_id=1, source_target_pairs={{0,1},{1,0},{2,3},{3,2},{4,5},{5,4},{6,7},{7,6},{8,9},{9,8},{10,11... | collective-permute-start | bytes 196616 | tf_op jit(solution)/shard_map/ppermute | solution.py:678
  28.0 4.7 %collective-permute-start.11 = (f32[128,128]{1,0:T(8,128)S(1)}, f32[128,128]{1,0:T(8,128)S(1)}, u32[]{:S(2)}, u32[]{:S(2)}) collective-permute-start(f32[128,128]{1,0:T(8,128)S(1)} %add.21), channel_id=1, source_target_pairs={{0,2},{1,3},{2,0},{3,1},{4,6},{5,7},{6,4},{7,5},{8,10},{9,11},{10,... | collective-permute-start | bytes 196616 | tf_op jit(solution)/shard_map/ppermute | solution.py:678
  32.6 5.2 %collective-permute-start.12 = (f32[128,128]{1,0:T(8,128)S(1)}, f32[128,128]{1,0:T(8,128)S(1)}, u32[]{:S(2)}, u32[]{:S(2)}) collective-permute-start(f32[128,128]{1,0:T(8,128)S(1)} %add.22), channel_id=1, source_target_pairs={{0,4},{1,5},{2,6},{3,7},{4,0},{5,1},{6,2},{7,3},{8,12},{9,13},{10,... | collective-permute-start | bytes 196616 | tf_op jit(solution)/shard_map/ppermute | solution.py:678

commit v3 on v2

--- a/solution.py
+++ b/solution.py
@@ -110,12 +110,13 @@
 
 def own_kernel(bits, tile_width, rows_ref, taps_ref, filter_ref, pair_ref, conv_ref, *refs):
     unit_refs, window = refs[:-1], refs[-1]
+    parts_out = len(unit_refs) // len(bits)
     length, width = rows_ref.shape[1:]
     half = width // 2
     me = lax.axis_index("seq")
     filter_high, filter_low = halves(filter_ref[...])
     put_filter(pair_ref, 4 * length, filter_high, filter_low)
-    for later in unit_refs[1::2]:
+    for later in unit_refs[1::parts_out]:
         put_filter(later, 2 * length, filter_high, filter_low)
     window[:, 0:EDGE] = jnp.zeros((3, EDGE, tile_width), F32)
     for tile in range(width // tile_width):
@@ -134,18 +135,22 @@
         lanes_half = slice(tile * tile_width % half, tile * tile_width % half + tile_width)
         for index, bit in enumerate(bits):
             low_side = (me // bit) % 2 == 0
-            first, later = unit_refs[2 * index : 2 * index + 2]
-            target_low, target_high = (first, later) if in_half == 0 else (later, first)
+            first, *laters = unit_refs[parts_out * index : parts_out * (index + 1)]
+            cut = laters[0].shape[1]
+            later = laters[lanes_half.start // cut]
+            lanes_later = slice(lanes_half.start % cut, lanes_half.start % cut + tile_width)
+            targets = [(first, lanes_half), (later, lanes_later)]
+            (low, lanes_low), (high, lanes_high) = targets if in_half == 0 else targets[::-1]
 
             @pl.when(low_side)
             def _():
-                target_low[0:length, lanes_half] = parts[0]
-                target_low[length : 2 * length, lanes_half] = parts[1]
+                low[0:length, lanes_low] = parts[0]
+                low[length : 2 * length, lanes_low] = parts[1]
 
             @pl.when(jnp.logical_not(low_side))
             def _():
-                target_high[0:length, lanes_half] = parts[2]
-                target_high[length : 2 * length, lanes_half] = parts[3]
+                high[0:length, lanes_high] = parts[2]
+                high[length : 2 * length, lanes_high] = parts[3]
 
 
 def first_kernel(marks_refs, taps_ref, own_marks, *refs):
@@ -333,7 +338,7 @@
     return jnp.where(row % 2 == 0, 1.0, -1.0)
 
 
-def result_kernel(blocks, tile_width, tiles, *refs):
+def result_kernel(blocks, tile_width, tiles, fresh_windows, *refs):
     others = blocks // 2 - 1
     (
         rows_ref,
@@ -351,7 +356,7 @@
     refs = refs[11:]
     units = [refs[4 * index : 4 * index + 4] for index in range(others)]
     refs = refs[4 * others :]
-    if tiles[0] == 0:
+    if fresh_windows:
         outs, (spectra, filter_rows) = refs[:4], refs[4:6]
         refs = refs[6:]
     else:
@@ -367,7 +372,7 @@
     core, chip = me % 2, me // 2
     forward, inverse = forward_ref[0 : 2 * length], inverse_ref[...]
 
-    if tiles[0] == 0:
+    if fresh_windows:
         sign = signs(length, groups)
         for edge in (0, 1, blocks + 2):
             filter_rows[edge] = jnp.zeros((length, groups), F32)
@@ -422,6 +427,8 @@
         in_half = start // half
         lanes = slice(start, start + tile_width)
         lanes_half = slice(start % half, start % half + tile_width)
+        place = start % half % units[0][1].shape[1]
+        lanes_later = slice(place, place + tile_width)
         lanes_out = slice(count * tile_width, (count + 1) * tile_width)
         weights = [taps_ref[p, :, lanes] for p in range(3)]
         fix[...] = jnp.zeros(fix.shape, F32)
@@ -441,19 +448,22 @@
             other = chip ^ (index + 1)
             for side in range(2):
                 first, later = unit[2 * side : 2 * side + 2]
-                body_low, body_high = (first, later) if in_half == 0 else (later, first)
+                bodies = [(first, lanes_half), (later, lanes_later)]
+                (body_low, lanes_low), (body_high, lanes_high) = (
+                    bodies if in_half == 0 else bodies[::-1]
+                )
                 block = 2 * other + (core if side == 0 else 1 - core)
 
                 @pl.when(other < chip)
                 def _():
                     signal = firsts_ref[block, 0, :, lanes]
-                    spec = spectrum(forward, margin, signal, body_low, 0, lanes_half)
+                    spec = spectrum(forward, margin, signal, body_low, 0, lanes_low)
                     add_lower(me - block, signal, spec)
 
                 @pl.when(other > chip)
                 def _():
                     signal = firsts_ref[block, 1, :, lanes]
-                    spec = spectrum(forward, margin, signal, body_high, 0, lanes_half)
+                    spec = spectrum(forward, margin, signal, body_high, 0, lanes_high)
                     add_upper(block - me, signal, spec)
 
         after_key, after_value, after_incoming = [
@@ -583,10 +593,15 @@
     filter_rows = length * groups // width
     pair_shape = shape((4 * length + 2 * filter_rows, width), BF16)
     first_shape = shape((2 * length, half), BF16)
-    later_shape = shape((2 * length + 4 * filter_rows, half), BF16)
+    half_tiles = half // tile_width
+    cut_tiles = (half_tiles + 1) // 2
+    cut = cut_tiles * tile_width
+    later_shapes = [shape((2 * length + 2 * length * groups // cut, cut), BF16)]
+    if cut < half:
+        later_shapes.append(shape((2 * length, half - cut), BF16))
     pair, conv, *own_units = call(
         functools.partial(own_kernel, bits, tile_width),
-        [pair_shape, shape((3, length, width), F32)] + [first_shape, later_shape] * len(bits),
+        [pair_shape, shape((3, length, width), F32)] + [first_shape, *later_shapes] * len(bits),
         [rows, short_taps, long_filter],
         [pltpu.VMEM((3, EDGE + length, tile_width), F32)],
         cost=40 * length * width,
@@ -601,7 +616,8 @@
             units.update(arrived)
         return [units[index] for index in range(1, chips)]
 
-    firsts = gather(own_units[0::2])
+    parts_out = 1 + len(later_shapes)
+    firsts = gather(own_units[0::parts_out])
     sibling = swap(pair, 1)
     spec, near = call(
         functools.partial(chip_kernel, tile_width, groups, margin),
@@ -622,28 +638,36 @@
         [spec, near, forward, inverse, *unit_specs],
         [pltpu.VMEM((blocks + 1, 2 * length, groups), F32)],
     )
-    laters = gather([after(unit, firsts_true) for unit in own_units[1::2]])
-    share, sent = shares[0] + swap(shares[1], 1), shares[2] + swap(shares[3], 1)
+    laters = [gather([after(unit, firsts_true) for unit in own_units[1::parts_out]])]
+    share = after(shares[0], *laters[0]) + swap(shares[1], 1)
+    sent = shares[2] + swap(shares[3], 1)
     for bit in bits:
-        share = after(share, *laters) + swap(sent, bit)
+        share = share + swap(sent, bit)
         if bit > 2:
             count = share.shape[0] // 2
             share, sent = share[:count], share[count:]
-    units = []
-    for first, later in zip(firsts, laters):
-        units += [first, later, swap(after(first, share), 1), swap(after(later, share), 1)]
+    if len(later_shapes) > 1:
+        laters.append(gather([after(unit, share) for unit in own_units[2::parts_out]]))
+    firsts_forwarded = [swap(after(first, share), 1) for first in firsts]
+
+    def units_of(part, behind):
+        units = []
+        for first, later, forwarded in zip(firsts, laters[part], firsts_forwarded):
+            units += [first, later, forwarded, swap(after(later, behind), 1)]
+        return units
+
     rows_out = shape((length, width), BF16)
     windows = [
         shape((blocks, 2 * length, groups), F32),
         shape((blocks + 3, length, groups), F32),
     ]
 
-    def results(tiles, extra, outs, out_specs):
+    def results(tiles, units, extra, outs, out_specs):
         args = [rows, short_taps, long_filter, conv, conv_first, firsts_true, after_rows]
         args += [sibling, spec, forward, inverse, *units]
         count = len(args)
         return call(
-            functools.partial(result_kernel, blocks, tile_width, tiles),
+            functools.partial(result_kernel, blocks, tile_width, tiles, not extra),
             outs,
             args + extra,
             [
@@ -659,27 +683,33 @@
             80 * length * len(tiles) * tile_width,
         )
 
-    tiles = width // tile_width
-    cuts = [0, max(1, tiles // 4), tiles - tiles // 4, tiles]
+    units = units_of(0, share)
     *final, spectra, filter_blocks = results(
-        range(cuts[0], cuts[1]), [], [rows_out] * 4 + windows, [HBM] * 4 + [VMEM] * 2
-    )
-    ready = [final]
-    for begin, end in zip(cuts[1:], cuts[2:]):
-        if begin < end:
-            final = results(
-                range(begin, end), [spectra, filter_blocks, *final], [rows_out] * 4, [HBM] * 4
-            )
-        ready.append(final)
-
+        range(cut_tiles), units, [], [rows_out] * 4 + windows, [HBM] * 4 + [VMEM] * 2
+    )
+
+    def more_results(final, tiles, units):
+        extra = [spectra, filter_blocks, *final]
+        return results(tiles, units, extra, [rows_out] * 4, [HBM] * 4)
+
+    later_tiles = [
+        in_half * half_tiles + tile for in_half in range(2) for tile in range(cut_tiles, half_tiles)
+    ]
     grad_filter = share[0]
+    ready = [final, more_results(final, range(half_tiles, half_tiles + cut_tiles), units)]
+
     steps = [1 << index for index in range(chans.bit_length() - 1)]
+    if len(laters) > 1 and len(steps) < 2:
+        ready.append(more_results(ready[1], later_tiles, units_of(1, grad_filter)))
     for index, step in enumerate(steps):
+        beside = index + 3 - len(steps)
         arrived = lax.ppermute(grad_filter, "chan", [(i, i ^ step) for i in range(chans)])
-        beside = index + len(ready) - len(steps)
-        if beside >= 0:
+        if beside == 1 and len(laters) > 1:
+            ready.append(more_results(ready[1], later_tiles, units_of(1, grad_filter)))
+        if 0 <= beside < len(ready):
             grad_filter = after(grad_filter, ready[beside][0])
         grad_filter = grad_filter + arrived
+    final = ready[-1]
     return (*final, grad_filter)
 
 

time: 38.7 us -> 40.1 us (1.036)
  waiting for transfers between devices: 10.5 us -> 11.3 us
  starting transfers between devices: 13.1 us -> 13.7 us
    ppermute x3, waiting for transfers between devices: 1.24 us -> 2.36 us  [per_device(): lax.ppermute(grad_filter, 'chan', [(i, i ^ step) for i in range(chans)])]
    ppermute x10 -> x12, starting transfers between devices: 7.3 us -> 7.93 us  [swap(): return lax.ppermute(block, 'seq', [(i, i ^ bit) for i in range(blocks)])]
    ppermute x10 -> x12, waiting for transfers between devices: 9.22 us -> 8.97 us  [swap(): return lax.ppermute(block, 'seq', [(i, i ^ bit) for i in range(blocks)])]
  transfers between devices with their start and end apart: 13 -> 15, of which waited for: 8 -> 10; matrix products, arithmetic and copies ran while one was open for 0% -> 0% of each run, Pallas kernels for 29% -> 27%
where the time goes in v3:
time: 40.1 us; the launch traced here: 39.9 us
  starting transfers between devices  13.7 us (34%)
  Pallas kernels  13.5 us (34%)
  waiting for transfers between devices  11.3 us (28%)
  between operations  0.75 us (2%)
  other arithmetic  0.68 us (2%)
    pallas_call x9, Pallas kernels, call(): pl.pallas_call(kernel, out_shape=outs, in_specs=in_specs or [VMEM] * len(...  13.5 us
    ppermute x12, waiting for transfers between devices, swap(): return lax.ppermute(block, 'seq', [(i, i ^ bit) for i in range(blocks)])  8.97 us
    ppermute x12, starting transfers between devices, swap(): return lax.ppermute(block, 'seq', [(i, i ^ bit) for i in range(blocks)])  7.93 us
    ppermute x3, starting transfers between devices, per_device(): lax.ppermute(grad_filter, 'chan', [(i, i ^ step) for i in range(chans)])  5.72 us
    ppermute x3, waiting for transfers between devices, per_device(): lax.ppermute(grad_filter, 'chan', [(i, i ^ step) for i in range(chans)])  2.36 us
  transfers between devices with their start and end apart: 15, of which 10 were waited for; matrix products, arithmetic and copies ran while one was open for 0% of the time, Pallas kernels for 27%

profile of v3, /device:TPU:0, one launch (start us, length us, event | category | flops | bytes accessed | tf_op | source)
XLA Modules:
  0.0 39.9 jit_solution(14986719928688954786)
XLA Ops:
  0.6 1.4 %shard_map.119 = (bf16[4,128,1024]{2,1,0:T(8,128)(2,1)S(1)}, bf16[16,1024]{1,0:T(8,128)(2,1)S(1)}, f32[3,3,1024]{2,1,0:T(4,128)S(1)}, f32[128,128]{1,0:T(8,128)S...) custom-call(bf16[128,1024]{1,0:T(8,128)(2,1)} %q_hbm.1, bf16[128,1024]{1,0:T(8,128)(2,1)} %k_hbm.1, ...), custom_call_target="tpu_custom_call" | custom-call | flops 1 | bytes 1 | tf_op jit(solution)/shard_map/pallas_call | solution.py:534
  2.1 1.1 %shard_map.120 = (bf16[544,1024]{1,0:T(8,128)(2,1)S(1)}, f32[3,128,1024]{2,1,0:T(8,128)S(1)}, bf16[256,512]{1,0:T(8,128)(2,1)S(1)}, bf16[384,256]{1,0:T(8,128)(2,1)S(1)}, bf16[256,256]{1,0:T(8,128)(2,1)S(1)}) custom-call(bf16[4,128,1024]{2,1,0:T(8,128)(2,1)S(1)} %get-tuple-element.49.rows_ref.refs_0_, f32[3,3,1024]{2,1,0:T(4,128)S(1)} %get-tuple-element.50.taps_ref.refs_1_, ...), custom_call_target="tpu_custom_call" | custom-call | flops 1 | bytes 5242880 | tf_op jit(solution)/shard_map/pallas_call | solution.py:534
  3.7 2.6 %collective-permute-start = (bf16[16,1024]{1,0:T(8,128)(2,1)S(1)}, bf16[16,1024]{1,0:T(8,128)(2,1)S(1)}, u32[]{:S(2)}, u32[]{:S(2)}) collective-permute-start(bf16[16,1024]{1,0:T(8,128)(2,1)S(1)} %get-tuple-element.53.own_marks), channel_id=1, source_target_pairs={{0,16},{8,24},{16,0},{24,8},{1,17},{9,25},{17,1},{25,9},{2,18},{10... | collective-permute-start | bytes 98312 | tf_op jit(solution)/shard_map/ppermute | solution.py:530
  6.4 1.9 %collective-permute-done.refs_0_ = bf16[16,1024]{1,0:T(8,128)(2,1)S(1)} collective-permute-done((bf16[16,1024]{1,0:T(8,128)(2,1)S(1)}, bf16[16,1024]{1,0:T(8,128)(2,1)S(1)}, u32[]{:S(2)}, u32[]{:S(2)}) %collective-permute-start) | collective-permute-done | bytes 32800 | tf_op jit(solution)/shard_map/ppermute | solution.py:530
  8.3 1.2 %collective-permute-done.1.refs_1_ = bf16[32,1024]{1,0:T(8,128)(2,1)S(1)} collective-permute-done((bf16[32,1024]{1,0:T(8,128)(2,1)S(1)}, bf16[32,1024]{1,0:T(8,128)(2,1)S(1)}, u32[]{:S(2)}, u32[]{:S(2)}) %collective-permute-start.1) | collective-permute-done | bytes 65568 | tf_op jit(solution)/shard_map/ppermute | solution.py:530
  9.9 2.3 %collective-permute-start.4 = (bf16[384,256]{1,0:T(8,128)(2,1)S(1)}, bf16[384,256]{1,0:T(8,128)(2,1)S(1)}, u32[]{:S(2)}, u32[]{:S(2)}) collective-permute-start(bf16[384,256]{1,0:T(8,128)(2,1)S(1)} %get-tuple-element.67), channel_id=1, source_target_pairs={{0,16},{8,24},{16,0},{24,8},{1,17},{9,25},{17,1},{25,9},{2,18},{10... | collective-permute-start | bytes 589832 | tf_op jit(solution)/shard_map/ppermute | solution.py:530
  12.2 2.4 %shard_map.122 = (f32[4,256,1024]{2,1,0:T(8,128)S(1)}, f32[2,256,128]{2,1,0:T(8,128)S(1)}) custom-call(bf16[544,1024]{1,0:T(8,128)(2,1)S(1)} %get-tuple-element.57.own_ref, bf16[544,1024]{1,0:T(8,128)(2,1)S(1)} %collective-permute-done.2.other_ref.refs_7_, f32[4,2,8,1024]{3,2,1,0:T(8,128)S(1)} %get-tuple-element.64.firsts_ref.refs_5_, ...), custom_call_target="tpu_custom_call" | custom-call | flops 1 | bytes 1 | tf_op jit(solution)/shard_map/pallas_call | solution.py:534
  14.6 0.9 %collective-permute-done.3.refs_0_.refs_11_ = bf16[256,512]{1,0:T(8,128)(2,1)S(1)} collective-permute-done((bf16[256,512]{1,0:T(8,128)(2,1)S(1)}, bf16[256,512]{1,0:T(8,128)(2,1)S(1)}, u32[]{:S(2)}, u32[]{:S(2)}) %collective-permute-start.3) | collective-permute-done | bytes 262176 | tf_op jit(solution)/shard_map/ppermute | solution.py:530
  15.8 0.8 %shard_map.124 = (f32[1,128,128]{2,1,0:T(8,128)S(1)}, f32[1,128,128]{2,1,0:T(8,128)S(1)}, f32[1,128,128]{2,1,0:T(8,128)S(1)}, f32[1,128,128]{2,1,0:T(8,128)S(1)}) custom-call(f32[4,256,1024]{2,1,0:T(8,128)S(1)} %get-tuple-element.59.spec_ref.refs_8_, f32[2,256,128]{2,1,0:T(8,128)S(1)} %get-tuple-element.63.near_ref, ...), custom_call_target="tpu_custom_call" | custom-call | flops 1 | bytes 1 | tf_op jit(solution)/shard_map/pallas_call | solution.py:534
  17.2 0.7 %collective-permute-done.6 = f32[1,128,128]{2,1,0:T(8,128)S(1)} collective-permute-done((f32[1,128,128]{2,1,0:T(8,128)S(1)}, f32[1,128,128]{2,1,0:T(8,128)S(1)}, u32[]{:S(2)}, u32[]{:S(2)}) %collective-permute-start.6) | collective-permute-done | bytes 65568 | tf_op jit(solution)/shard_map/ppermute | solution.py:530
  17.9 0.7 %collective-permute-start.7 = (f32[1,128,128]{2,1,0:T(8,128)S(1)}, f32[1,128,128]{2,1,0:T(8,128)S(1)}, u32[]{:S(2)}, u32[]{:S(2)}) collective-permute-start(f32[1,128,128]{2,1,0:T(8,128)S(1)} %add.19), channel_id=1, source_target_pairs={{0,16},{8,24},{16,0},{24,8},{1,17},{9,25},{17,1},{25,9},{2,18},{10... | collective-permute-start | bytes 196616 | tf_op jit(solution)/shard_map/ppermute | solution.py:530
  18.9 3.4 %collective-permute-done.7 = f32[1,128,128]{2,1,0:T(8,128)S(1)} collective-permute-done((f32[1,128,128]{2,1,0:T(8,128)S(1)}, f32[1,128,128]{2,1,0:T(8,128)S(1)}, u32[]{:S(2)}, u32[]{:S(2)}) %collective-permute-start.7) | collective-permute-done | bytes 65568 | tf_op jit(solution)/shard_map/ppermute | solution.py:530
  22.9 0.6 %collective-permute-start.8 = (bf16[256,256]{1,0:T(8,128)(2,1)S(1)}, bf16[256,256]{1,0:T(8,128)(2,1)S(1)}, u32[]{:S(2)}, u32[]{:S(2)}) collective-permute-start(bf16[256,256]{1,0:T(8,128)(2,1)S(1)} %get-tuple-element.72), channel_id=1, source_target_pairs={{0,16},{8,24},{16,0},{24,8},{1,17},{9,25},{17,1},{25,9},{2,18},{10... | collective-permute-start | bytes 393224 | tf_op jit(solution)/shard_map/ppermute | solution.py:530
  23.5 1.5 %collective-permute-start.11 = (f32[128,128]{1,0:T(8,128)S(1)}, f32[128,128]{1,0:T(8,128)S(1)}, u32[]{:S(2)}, u32[]{:S(2)}) collective-permute-start(f32[128,128]{1,0:T(8,128)S(1)} %bitcast.1), channel_id=1, source_target_pairs={{0,1},{1,0},{2,3},{3,2},{4,5},{5,4},{6,7},{7,6},{8,9},{9,8},{10,11... | collective-permute-start | bytes 196616 | tf_op jit(solution)/shard_map/ppermute | solution.py:706
  25.0 2.2 %shard_map.125 = (bf16[128,1024]{1,0:T(8,128)(2,1)}, bf16[128,1024]{1,0:T(8,128)(2,1)}, bf16[128,1024]{1,0:T(8,128)(2,1)}, bf16[128,1024]{1,0:T(8,128)(2,1)}, f3...) custom-call(bf16[4,128,1024]{2,1,0:T(8,128)(2,1)S(1)} %get-tuple-element.49.rows_ref.refs_0_, ...), custom_call_target="tpu_custom_call" | custom-call | flops 1 | bytes 2621440 | tf_op jit(solution)/shard_map/pallas_call | solution.py:534
  27.2 0.6 %collective-permute-done.11 = f32[128,128]{1,0:T(8,128)S(1)} collective-permute-done((f32[128,128]{1,0:T(8,128)S(1)}, f32[128,128]{1,0:T(8,128)S(1)}, u32[]{:S(2)}, u32[]{:S(2)}) %collective-permute-start.11) | collective-permute-done | bytes 65568 | tf_op jit(solution)/shard_map/ppermute | solution.py:706
  27.8 0.6 %collective-permute-done.8.refs_12_ = bf16[256,256]{1,0:T(8,128)(2,1)S(1)} collective-permute-done((bf16[256,256]{1,0:T(8,128)(2,1)S(1)}, bf16[256,256]{1,0:T(8,128)(2,1)S(1)}, u32[]{:S(2)}, u32[]{:S(2)}) %collective-permute-start.8) | collective-permute-done | bytes 131104 | tf_op jit(solution)/shard_map/ppermute | solution.py:530
  28.3 1.6 %collective-permute-start.13 = (f32[128,128]{1,0:T(8,128)S(1)}, f32[128,128]{1,0:T(8,128)S(1)}, u32[]{:S(2)}, u32[]{:S(2)}) collective-permute-start(f32[128,128]{1,0:T(8,128)S(1)} %add.21), channel_id=1, source_target_pairs={{0,2},{1,3},{2,0},{3,1},{4,6},{5,7},{6,4},{7,5},{8,10},{9,11},{10,... | collective-permute-start | bytes 196616 | tf_op jit(solution)/shard_map/ppermute | solution.py:706
  29.9 1.9 %shard_map.126 = (bf16[128,1024]{1,0:T(8,128)(2,1)}, bf16[128,1024]{1,0:T(8,128)(2,1)}, bf16[128,1024]{1,0:T(8,128)(2,1)}, bf16[128,1024]{1,0:T(8,128)(2,1)}) custom-call(bf16[4,128,1024]{2,1,0:T(8,128)(2,1)S(1)} %get-tuple-element.49.rows_ref.refs_0_, ...), custom_call_target="tpu_custom_call", output_to_operand_aliasing={{0}: (17, {}), {1}: (18, {}), {2}: (19, {}), {3}: (20, {})} | custom-call | flops 1 | bytes 2621440 | tf_op jit(solution)/shard_map/pallas_call | solution.py:534
  31.8 1.0 %collective-permute-done.13 = f32[128,128]{1,0:T(8,128)S(1)} collective-permute-done((f32[128,128]{1,0:T(8,128)S(1)}, f32[128,128]{1,0:T(8,128)S(1)}, u32[]{:S(2)}, u32[]{:S(2)}) %collective-permute-start.13) | collective-permute-done | bytes 65568 | tf_op jit(solution)/shard_map/ppermute | solution.py:706
  32.9 2.7 %collective-permute-start.14 = (f32[128,128]{1,0:T(8,128)S(1)}, f32[128,128]{1,0:T(8,128)S(1)}, u32[]{:S(2)}, u32[]{:S(2)}) collective-permute-start(f32[128,128]{1,0:T(8,128)S(1)} %add.22), channel_id=1, source_target_pairs={{0,4},{1,5},{2,6},{3,7},{4,0},{5,1},{6,2},{7,3},{8,12},{9,13},{10,... | collective-permute-start | bytes 196616 | tf_op jit(solution)/shard_map/ppermute | solution.py:706
  35.5 3.0 %shard_map.127 = (bf16[128,1024]{1,0:T(8,128)(2,1)}, bf16[128,1024]{1,0:T(8,128)(2,1)}, bf16[128,1024]{1,0:T(8,128)(2,1)}, bf16[128,1024]{1,0:T(8,128)(2,1)}) custom-call(bf16[4,128,1024]{2,1,0:T(8,128)(2,1)S(1)} %get-tuple-element.49.rows_ref.refs_0_, ...), custom_call_target="tpu_custom_call", output_to_operand_aliasing={{0}: (17, {}), {1}: (18, {}), {2}: (19, {}), {3}: (20, {})} | custom-call | flops 1 | bytes 5242880 | tf_op jit(solution)/shard_map/pallas_call | solution.py:534
  38.5 0.7 %collective-permute-done.14 = f32[128,128]{1,0:T(8,128)S(1)} collective-permute-done((f32[128,128]{1,0:T(8,128)S(1)}, f32[128,128]{1,0:T(8,128)S(1)}, u32[]{:S(2)}, u32[]{:S(2)}) %collective-permute-start.14) | collective-permute-done | bytes 65568 | tf_op jit(solution)/shard_map/ppermute | solution.py:706
  39.3 0.6 %add.23 = f32[128,128]{1,0:T(8,128)} add(f32[128,128]{1,0:T(8,128)S(1)} %add.22, f32[128,128]{1,0:T(8,128)S(1)} %collective-permute-done.14) | non-fusion elementwise | flops 16384 | bytes 196608 | tf_op jit(solution)/shard_map/add | solution.py:711
  (21 shorter events, 2.8 us)
Async XLA Ops:
  3.2 9.0 %collective-permute-start.2 = (bf16[544,1024]{1,0:T(8,128)(2,1)S(1)}, bf16[544,1024]{1,0:T(8,128)(2,1)S(1)}, u32[]{:S(2)}, u32[]{:S(2)}) collective-permute-start(bf16[544,1024]{1,0:T(8,128)(2,1)S(1)} %get-tuple-element.57.own_ref), channel_id=1, source_target_pairs={{0,8},{8,0},{16,24},{24,16},{1,9},{9,1},{17,25},{25,17},{2,10},{10... | collective-permute-start | bytes 3342344 | tf_op jit(solution)/shard_map/ppermute | solution.py:530
  3.7 4.6 %collective-permute-start = (bf16[16,1024]{1,0:T(8,128)(2,1)S(1)}, bf16[16,1024]{1,0:T(8,128)(2,1)S(1)}, u32[]{:S(2)}, u32[]{:S(2)}) collective-permute-start(bf16[16,1024]{1,0:T(8,128)(2,1)S(1)} %get-tuple-element.53.own_marks), channel_id=1, source_target_pairs={{0,16},{8,24},{16,0},{24,8},{1,17},{9,25},{17,1},{25,9},{2,18},{10... | collective-permute-start | bytes 98312 | tf_op jit(solution)/shard_map/ppermute | solution.py:530
  6.3 9.2 %collective-permute-start.3 = (bf16[256,512]{1,0:T(8,128)(2,1)S(1)}, bf16[256,512]{1,0:T(8,128)(2,1)S(1)}, u32[]{:S(2)}, u32[]{:S(2)}) collective-permute-start(bf16[256,512]{1,0:T(8,128)(2,1)S(1)} %get-tuple-element.61), channel_id=1, source_target_pairs={{0,16},{8,24},{16,0},{24,8},{1,17},{9,25},{17,1},{25,9},{2,18},{10... | collective-permute-start | bytes 786440 | tf_op jit(solution)/shard_map/ppermute | solution.py:530
  8.3 1.3 %collective-permute-start.1 = (bf16[32,1024]{1,0:T(8,128)(2,1)S(1)}, bf16[32,1024]{1,0:T(8,128)(2,1)S(1)}, u32[]{:S(2)}, u32[]{:S(2)}) collective-permute-start(bf16[32,1024]{1,0:T(8,128)(2,1)S(1)} %pad_maximum_fusion), channel_id=1, source_target_pairs={{0,8},{8,0},{16,24},{24,16},{1,9},{9,1},{17,25},{25,17},{2,10},{10... | collective-permute-start | bytes 196616 | tf_op jit(solution)/shard_map/ppermute | solution.py:530
  9.9 9.0 %collective-permute-start.4 = (bf16[384,256]{1,0:T(8,128)(2,1)S(1)}, bf16[384,256]{1,0:T(8,128)(2,1)S(1)}, u32[]{:S(2)}, u32[]{:S(2)}) collective-permute-start(bf16[384,256]{1,0:T(8,128)(2,1)S(1)} %get-tuple-element.67), channel_id=1, source_target_pairs={{0,16},{8,24},{16,0},{24,8},{1,17},{9,25},{17,1},{25,9},{2,18},{10... | collective-permute-start | bytes 589832 | tf_op jit(solution)/shard_map/ppermute | solution.py:530
  16.6 1.3 %collective-permute-start.6 = (f32[1,128,128]{2,1,0:T(8,128)S(1)}, f32[1,128,128]{2,1,0:T(8,128)S(1)}, u32[]{:S(2)}, u32[]{:S(2)}) collective-permute-start(f32[1,128,128]{2,1,0:T(8,128)S(1)} %get-tuple-element.71), channel_id=1, source_target_pairs={{0,8},{8,0},{16,24},{24,16},{1,9},{9,1},{17,25},{25,17},{2,10},{10... | collective-permute-start | bytes 196616 | tf_op jit(solution)/shard_map/ppermute | solution.py:530
  16.7 2.2 %collective-permute-start.5 = (f32[1,128,128]{2,1,0:T(8,128)S(1)}, f32[1,128,128]{2,1,0:T(8,128)S(1)}, u32[]{:S(2)}, u32[]{:S(2)}) collective-permute-start(f32[1,128,128]{2,1,0:T(8,128)S(1)} %get-tuple-element.69), channel_id=1, source_target_pairs={{0,8},{8,0},{16,24},{24,16},{1,9},{9,1},{17,25},{25,17},{2,10},{10... | collective-permute-start | bytes 196616 | tf_op jit(solution)/shard_map/ppermute | solution.py:530
  17.9 4.3 %collective-permute-start.7 = (f32[1,128,128]{2,1,0:T(8,128)S(1)}, f32[1,128,128]{2,1,0:T(8,128)S(1)}, u32[]{:S(2)}, u32[]{:S(2)}) collective-permute-start(f32[1,128,128]{2,1,0:T(8,128)S(1)} %add.19), channel_id=1, source_target_pairs={{0,16},{8,24},{16,0},{24,8},{1,17},{9,25},{17,1},{25,9},{2,18},{10... | collective-permute-start | bytes 196616 | tf_op jit(solution)/shard_map/ppermute | solution.py:530
  22.3 2.7 %collective-permute-start.9 = (bf16[256,512]{1,0:T(8,128)(2,1)S(1)}, bf16[256,512]{1,0:T(8,128)(2,1)S(1)}, u32[]{:S(2)}, u32[]{:S(2)}) collective-permute-start(bf16[256,512]{1,0:T(8,128)(2,1)S(1)} %collective-permute-done.3.refs_0_.refs_11_), channel_id=1, source_target_pairs={{0,8},{8,0},{16,24},{24,16},{1,9},{9,1},{17,25},{25,17},{2,10},{10... | collective-permute-start | bytes 786440 | tf_op jit(solution)/shard_map/ppermute | solution.py:530
  22.4 2.6 %collective-permute-start.10 = (bf16[384,256]{1,0:T(8,128)(2,1)S(1)}, bf16[384,256]{1,0:T(8,128)(2,1)S(1)}, u32[]{:S(2)}, u32[]{:S(2)}) collective-permute-start(bf16[384,256]{1,0:T(8,128)(2,1)S(1)} %collective-permute-done.4.refs_12_), channel_id=1, source_target_pairs={{0,8},{8,0},{16,24},{24,16},{1,9},{9,1},{17,25},{25,17},{2,10},{10... | collective-permute-start | bytes 589832 | tf_op jit(solution)/shard_map/ppermute | solution.py:530
  22.9 5.5 %collective-permute-start.8 = (bf16[256,256]{1,0:T(8,128)(2,1)S(1)}, bf16[256,256]{1,0:T(8,128)(2,1)S(1)}, u32[]{:S(2)}, u32[]{:S(2)}) collective-permute-start(bf16[256,256]{1,0:T(8,128)(2,1)S(1)} %get-tuple-element.72), channel_id=1, source_target_pairs={{0,16},{8,24},{16,0},{24,8},{1,17},{9,25},{17,1},{25,9},{2,18},{10... | collective-permute-start | bytes 393224 | tf_op jit(solution)/shard_map/ppermute | solution.py:530
  23.5 4.3 %collective-permute-start.11 = (f32[128,128]{1,0:T(8,128)S(1)}, f32[128,128]{1,0:T(8,128)S(1)}, u32[]{:S(2)}, u32[]{:S(2)}) collective-permute-start(f32[128,128]{1,0:T(8,128)S(1)} %bitcast.1), channel_id=1, source_target_pairs={{0,1},{1,0},{2,3},{3,2},{4,5},{5,4},{6,7},{7,6},{8,9},{9,8},{10,11... | collective-permute-start | bytes 196616 | tf_op jit(solution)/shard_map/ppermute | solution.py:706
  28.3 7.2 %collective-permute-start.12 = (bf16[256,256]{1,0:T(8,128)(2,1)S(1)}, bf16[256,256]{1,0:T(8,128)(2,1)S(1)}, u32[]{:S(2)}, u32[]{:S(2)}) collective-permute-start(bf16[256,256]{1,0:T(8,128)(2,1)S(1)} %collective-permute-done.8.refs_12_), channel_id=1, source_target_pairs={{0,8},{8,0},{16,24},{24,16},{1,9},{9,1},{17,25},{25,17},{2,10},{10... | collective-permute-start | bytes 393224 | tf_op jit(solution)/shard_map/ppermute | solution.py:530
  28.3 4.5 %collective-permute-start.13 = (f32[128,128]{1,0:T(8,128)S(1)}, f32[128,128]{1,0:T(8,128)S(1)}, u32[]{:S(2)}, u32[]{:S(2)}) collective-permute-start(f32[128,128]{1,0:T(8,128)S(1)} %add.21), channel_id=1, source_target_pairs={{0,2},{1,3},{2,0},{3,1},{4,6},{5,7},{6,4},{7,5},{8,10},{9,11},{10,... | collective-permute-start | bytes 196616 | tf_op jit(solution)/shard_map/ppermute | solution.py:706
  32.9 6.4 %collective-permute-start.14 = (f32[128,128]{1,0:T(8,128)S(1)}, f32[128,128]{1,0:T(8,128)S(1)}, u32[]{:S(2)}, u32[]{:S(2)}) collective-permute-start(f32[128,128]{1,0:T(8,128)S(1)} %add.22), channel_id=1, source_target_pairs={{0,4},{1,5},{2,6},{3,7},{4,0},{5,1},{6,2},{7,3},{8,12},{9,13},{10,... | collective-permute-start | bytes 196616 | tf_op jit(solution)/shard_map/ppermute | solution.py:706
